TPU v7x, 128 devices: a whole 4x4x4 slice. The times are simulated.
128 devices in a mesh: lat: 8 (over z, core), lon: 16 (over y, x).
Axes of the slice: x: 4, y: 4, z: 4, core: 2. Of those that a mesh axis runs over, the one named last changes fastest.
Arguments:
- grid: bfloat16 [360, 1440, 256], P('lat', 'lon'), may hold values from -6 to 6
- dw_kernel: bfloat16 [1, 7, 7, 256], replicated, may hold values from -0.875 to 0.875
- norm_gain: float32 [1, 256], replicated, may hold values from 0.25 to 1.75
- w_up: bfloat16 [1, 256, 512], replicated, may hold values from -0.375 to 0.375
- w_down: bfloat16 [1, 512, 256], replicated, may hold values from -0.25 to 0.25
- w_read: bfloat16 [256, 64], replicated, may hold values from -0.375 to 0.375
- owner: int32 [1048576, 1], P(('lat', 'lon')), may hold values from 0 to 127; in each aligned block of 8192 rows (0 to 8191, 8192 to 16383, ...) at most 128 rows name the same one
- offsets: int32 [1048576], P(('lat', 'lon')), may hold values from 0 to 4049
- fractions: float32 [2, 1048576], P(None, ('lat', 'lon')), may hold values from 0 to 1
Outputs:
- readout: bfloat16 [1048576, 64], P(('lat', 'lon'))
Inputs may be any that keep to these rules, and one draw needn't show every extreme that they name: `owner`: among the targets of one device (8192 rows in a row), no tile owns more than 128; some tile owns exactly 128.
All inputs are finite; a program needn't handle non-finite values.
Results may differ from a plain program's by a relative error of at most 0.0055.
Values may be sent and summed in bfloat16 or wider, within the bound.
A program may use at most 192 MiB of HBM per device.

v0:
```python
import jax
import jax.numpy as jnp
from jax import lax
from jax.sharding import PartitionSpec as P


def extended_2(x, sides, width):
    for axis, dim in sides:
        size, length = (lax.axis_size(axis), x.shape[dim])
        up = [(i, (i + 1) % size) for i in range(size)]
        down = [(j, i) for i, j in up]
        last = lax.slice_in_dim(x, length - width, length, axis=dim)
        leading = lax.slice_in_dim(x, 0, width, axis=dim)
        before = lax.ppermute(last, axis, up)
        after = lax.ppermute(leading, axis, down)
        x = jnp.concatenate([before, x, after], axis=dim)
    return x


def conv_block(extended, kernel, gain, weight_up, weight_down):
    height = extended.shape[0] - 6
    breadth = extended.shape[1] - 6
    wide = extended.astype(jnp.float32)
    kernel_wide = kernel.astype(jnp.float32)
    summed = jnp.zeros((height, breadth, extended.shape[2]), jnp.float32)
    for shift_row in range(7):
        row_sum = wide[shift_row : shift_row + height, 0:breadth] * kernel_wide[shift_row, 0]
        for shift_col in range(1, 7):
            row_sum = (
                row_sum
                + wide[shift_row : shift_row + height, shift_col : shift_col + breadth]
                * kernel_wide[shift_row, shift_col]
            )
        summed = summed + row_sum
    centre_mean = jnp.mean(summed, axis=-1, keepdims=True)
    centred = summed - centre_mean
    variance = jnp.mean(centred * centred, axis=-1, keepdims=True)
    normed = (centred * lax.rsqrt(variance + 1e-06) * gain).astype(jnp.bfloat16)
    flattened = normed.reshape(height * breadth, -1)
    hidden = jax.nn.gelu(jnp.dot(flattened, weight_up, preferred_element_type=jnp.float32)).astype(
        jnp.bfloat16
    )
    delta = jnp.dot(hidden, weight_down, preferred_element_type=jnp.float32)
    centre = wide[3 : 3 + height, 3 : 3 + breadth].reshape(height * breadth, -1)
    return (centre + delta).astype(jnp.bfloat16).reshape(height, breadth, -1)


def windowed_table(tile):
    span = tile.shape[1] - 3
    pieces = [tile[:, shift_col : shift_col + span] for shift_col in range(4)]
    return (jnp.concatenate(pieces, axis=2).reshape(-1, 4 * tile.shape[2]), span)


def read_cells(windowed, span, width, base_row, base_col, frac_y, frac_x):
    shape = base_row.shape
    rows_flat = base_row.reshape(-1)
    cols_flat = base_col.reshape(-1)
    fy = frac_y.reshape(-1)
    fx = frac_x.reshape(-1)
    count = rows_flat.shape[0]
    summed = jnp.zeros((count, width), jnp.float32)
    weight_total = jnp.zeros((count,), jnp.float32)
    for step_row in range(-1, 3):
        position = ((rows_flat + step_row + 2) * span + cols_flat + 1).astype(jnp.int32)
        gathered = windowed[position].reshape(count, 4, width)
        weight = jnp.stack(
            [
                jnp.exp(-((fy - step_row) ** 2 + (fx - step_col) ** 2) * 0.5)
                for step_col in range(-1, 3)
            ],
            axis=-1,
        )
        summed = summed + jnp.sum(weight[:, :, None] * gathered.astype(jnp.float32), axis=1)
        weight_total = weight_total + jnp.sum(weight, axis=1)
    result = (summed / weight_total[:, None]).astype(jnp.bfloat16)
    return result.reshape(shape + (width,))


def mask_rows(field, first_row, total_rows):
    global_rows = first_row + jnp.arange(field.shape[0], dtype=jnp.int32)
    inside = (global_rows >= 0) & (global_rows < total_rows)
    return jnp.where(inside[:, None, None], field, jnp.zeros_like(field))


def shards(grid, dw_kernel, norm_gain, w_up, w_down, w_read, owner, offsets, fractions):
    tile_rows = grid.shape[0]
    tile_cols = grid.shape[1]
    out_width = w_read.shape[1]
    total_rows = tile_rows * lax.axis_size("lat")
    first_row = lax.axis_index("lat") * tile_rows
    field = grid
    extended = extended_2(field, (("lat", 0), ("lon", 1)), 3)
    extended = mask_rows(extended, first_row - 3, total_rows)
    field = conv_block(extended, dw_kernel[0], norm_gain[0], w_up[0], w_down[0])
    projected = jnp.dot(
        field.reshape(-1, field.shape[2]), w_read, preferred_element_type=jnp.float32
    ).astype(jnp.bfloat16)
    projected = projected.reshape(tile_rows, tile_cols, out_width)
    projected = extended_2(projected, (("lat", 0), ("lon", 1)), 2)
    projected = mask_rows(projected, first_row - 2, total_rows)
    windowed, span = windowed_table(projected)
    devices = lax.axis_size(("lat", "lon"))
    target_count = owner.shape[0]
    capacity = 2 * target_count // devices
    tiles = owner[:, 0]
    onehot = (tiles[:, None] == jnp.arange(devices, dtype=jnp.int32)[None, :]).astype(jnp.float32)
    blocked = onehot.reshape(target_count // 128, 128, devices)
    lower = (
        jnp.arange(128, dtype=jnp.int32)[:, None] > jnp.arange(128, dtype=jnp.int32)[None, :]
    ).astype(jnp.float32)
    within = jnp.einsum("ij,bjd->bid", lower, blocked, precision=lax.Precision.HIGHEST)
    block_sums = jnp.sum(blocked, axis=1)
    before = jnp.cumsum(block_sums, axis=0) - block_sums
    ranks = (within + before[:, None, :]).reshape(target_count, devices)
    slots = jnp.sum(ranks * onehot, axis=1).astype(jnp.int32)
    destination = tiles * capacity + slots
    offset_buffer = (
        jnp.zeros((devices * capacity,), jnp.int32)
        .at[destination]
        .set(offsets)
        .reshape(devices, capacity)
    )
    rowfrac_buffer = (
        jnp.zeros((devices * capacity,), jnp.float32)
        .at[destination]
        .set(fractions[0])
        .reshape(devices, capacity)
    )
    colfrac_buffer = (
        jnp.zeros((devices * capacity,), jnp.float32)
        .at[destination]
        .set(fractions[1])
        .reshape(devices, capacity)
    )
    cell_ids = lax.all_to_all(
        offset_buffer, ("lat", "lon"), split_axis=0, concat_axis=0, tiled=True
    )
    values = read_cells(
        windowed,
        span,
        out_width,
        cell_ids // tile_cols,
        cell_ids % tile_cols,
        lax.all_to_all(rowfrac_buffer, ("lat", "lon"), split_axis=0, concat_axis=0, tiled=True),
        lax.all_to_all(colfrac_buffer, ("lat", "lon"), split_axis=0, concat_axis=0, tiled=True),
    )
    item_count = values.shape[1]
    returned_flat = lax.all_to_all(
        values.reshape(values.shape[0], -1), ("lat", "lon"), split_axis=0, concat_axis=0, tiled=True
    )
    returned = returned_flat.reshape(values.shape[0], item_count, out_width)
    return returned.reshape(devices * capacity, out_width)[destination]


def solution(mesh):
    return jax.shard_map(
        shards,
        mesh=mesh,
        in_specs=(
            P("lat", "lon", None),
            P(),
            P(),
            P(),
            P(),
            P(),
            P(("lat", "lon"), None),
            P(("lat", "lon")),
            P(None, ("lat", "lon")),
        ),
        out_specs=P(("lat", "lon"), None),
        check_vma=False,
    )
```

profile of v0, /device:TPU:1, one launch (start us, length us, event | category | flops | bytes accessed | tf_op | source)
XLA Modules:
  0.0 709.6 jit_solution(13280288767637536726)
XLA Ops:
  9.0 31.2 %scatter_custom_fusion.2 = s32[16384]{0:T(1024)} fusion(s32[8192]{0:T(1024)S(1)} %bitcast.165, s32[8192]{0:T(1024)} %param.16, s32[]{:T(128)} %constant.35.clone.1), kind=kCustom, calls=%fused_computation.178 | custom fusion | bytes 66048 | tf_op jit(solution)/shard_map/scatter | solution.py:120
  40.2 10.2 %all-to-all-start.2 = ((s32[128,1,128]{2,1,0:T(1,128)}), s32[128,1,128]{2,1,0:T(1,128)S(1)}, u32[]{:S(2)}, u32[]{:S(2)}) async-start(s32[128,1,128]{2,1,0:T(1,128)} %bitcast.73), calls=%async_computation.2 | async-start | bytes 131072 | tf_op jit(solution)/shard_map/all_to_all | solution.py:135
  52.4 31.0 %scatter_custom_fusion.1 = f32[16384]{0:T(1024)} fusion(s32[8192]{0:T(1024)S(1)} %bitcast.166, f32[8192]{0:T(1024)S(1)} %bitcast.171, f32[]{:T(128)} %constant.32.clone.1), kind=kCustom, calls=%fused_computation.180 | custom fusion | bytes 65540 | tf_op jit(solution)/shard_map/scatter | solution.py:132
  83.4 31.0 %scatter_custom_fusion = f32[16384]{0:T(1024)} fusion(s32[8192]{0:T(1024)S(1)} %bitcast.167, f32[8192]{0:T(1024)S(1)} %bitcast.170, f32[]{:T(128)} %constant.32.clone.1), kind=kCustom, calls=%fused_computation.182 | custom fusion | bytes 65540 | tf_op jit(solution)/shard_map/scatter | solution.py:126
  115.0 9.8 %all-to-all-start.1 = ((f32[128,1,128]{2,1,0:T(1,128)}), f32[128,1,128]{2,1,0:T(1,128)S(1)}, u32[]{:S(2)}, u32[]{:S(2)}) async-start(f32[128,1,128]{2,1,0:T(1,128)} %bitcast.9), calls=%async_computation.1 | async-start | bytes 131072 | tf_op jit(solution)/shard_map/all_to_all | solution.py:145
  125.5 8.9 %all-to-all-done.1 = f32[128,1,128]{2,1,0:T(1,128)S(1)} async-done(((f32[128,1,128]{2,1,0:T(1,128)}), f32[128,1,128]{2,1,0:T(1,128)S(1)}, u32[]{:S(2)}, u32[]{:S(2)}) %all-to-all-start.1) | async-done | bytes 65568 | tf_op jit(solution)/shard_map/all_to_all | solution.py:145
  139.2 9.2 %all-to-all-done = f32[128,1,128]{2,1,0:T(1,128)S(1)} async-done(((f32[128,1,128]{2,1,0:T(1,128)}), f32[128,1,128]{2,1,0:T(1,128)S(1)}, u32[]{:S(2)}, u32[]{:S(2)}) %all-to-all-start) | async-done | bytes 65568 | tf_op jit(solution)/shard_map/all_to_all | solution.py:144
  164.6 30.0 %fusion.78 = (f32[45,90]{1,0:T(8,128)S(1)}, f32[45,90,256]{2,1,0:T(8,128)}) fusion(f32[256]{0:T(256)S(1)} %bitcast.173, f32[51,96,256]{2,1,0:T(8,128)S(1)} %fusion.59, f32[256]{0:T(256)S(1)} %bitcast.174, f32[256]{0:T(256)S(1)} %bitcast.175, f32[256]{0:T(256)S(1)} %bitcast.176, f32[256]{0:T(256)S(1)} %bitcast.177, f32[256]{0:T(256)S(1)} %bitcast.178, ...), kind=kLoop, calls=%fused_computation.197 | loop fusion | flops 101602352 | bytes 207426368 | tf_op jit(solution)/shard_map/reduce_sum | solution.py:35
  254.0 65.2 %gather_fusion = bf16[16384,256]{1,0:T(8,128)(2,1)} fusion(bf16[4459,256]{1,0:T(8,128)(2,1)S(1)} %copy.44, s32[16384]{0:T(1024)S(1)} %broadcast_clamp_fusion.3), kind=kCustom, calls=%fused_computation | custom fusion | bytes 16842752 | tf_op jit(solution)/shard_map/gather | solution.py:65
  319.2 12.3 %copy.31 = f32[16384,256]{0,1:T(8,128)} copy(bf16[16384,256]{1,0:T(8,128)(2,1)} %gather_fusion) | data formatting | bytes 25165824 | tf_op jit(solution)/shard_map/convert_element_type | solution.py:73
  331.5 65.2 %gather_fusion.1 = bf16[16384,256]{1,0:T(8,128)(2,1)} fusion(bf16[4459,256]{1,0:T(8,128)(2,1)S(1)} %copy.44, s32[16384]{0:T(1024)S(1)} %broadcast_clamp_fusion.2), kind=kCustom, calls=%fused_computation.1 | custom fusion | bytes 16842752 | tf_op jit(solution)/shard_map/gather | solution.py:65
  396.6 12.3 %copy.34 = f32[16384,256]{0,1:T(8,128)} copy(bf16[16384,256]{1,0:T(8,128)(2,1)} %gather_fusion.1) | data formatting | bytes 25165824 | tf_op jit(solution)/shard_map/convert_element_type | solution.py:73
  408.9 65.1 %gather_fusion.2 = bf16[16384,256]{1,0:T(8,128)(2,1)} fusion(bf16[4459,256]{1,0:T(8,128)(2,1)S(1)} %copy.44, s32[16384]{0:T(1024)S(1)} %broadcast_clamp_fusion.1), kind=kCustom, calls=%fused_computation.2 | custom fusion | bytes 16842752 | tf_op jit(solution)/shard_map/gather | solution.py:65
  474.1 12.3 %copy.36 = f32[16384,256]{0,1:T(8,128)} copy(bf16[16384,256]{1,0:T(8,128)(2,1)} %gather_fusion.2) | data formatting | bytes 25165824 | tf_op jit(solution)/shard_map/convert_element_type | solution.py:73
  486.4 65.2 %gather_fusion.3 = bf16[16384,256]{1,0:T(8,128)(2,1)} fusion(bf16[4459,256]{1,0:T(8,128)(2,1)S(1)} %copy.44, s32[16384]{0:T(1024)S(1)} %broadcast_clamp_fusion), kind=kCustom, calls=%fused_computation.3 | custom fusion | bytes 16842752 | tf_op jit(solution)/shard_map/gather | solution.py:65
  551.5 12.4 %copy.38 = f32[16384,256]{0,1:T(8,128)} copy(bf16[16384,256]{1,0:T(8,128)(2,1)} %gather_fusion.3) | data formatting | bytes 25165824 | tf_op jit(solution)/shard_map/convert_element_type | solution.py:73
  563.9 12.5 %multiply_reduce_fusion.2 = (f32[16384,64]{0,1:T(8,128)S(1)}, f32[16384,64]{0,1:T(8,128)S(1)}) fusion(f32[16384,4,64]{0,2,1:T(8,128)} %bitcast.138, f32[16384,4]{0,1:T(4,128)S(1)} %copy-done.7, f32[16384,4,64]{0,2,1:T(8,128)} %bitcast.136, f32[16384,4]{0,1:T(4,128)S(1)} %copy-done.5), kind=kLoop, calls=%fused_computation.10 | loop fusion | flops 14680064 | bytes 42467328 | tf_op jit(solution)/shard_map/reduce_sum | solution.py:73
  576.5 14.7 %multiply_reduce_fusion = (f32[16384,64]{0,1:T(8,128)S(1)}, f32[16384,64]{0,1:T(8,128)}) fusion(f32[16384,4,64]{0,2,1:T(8,128)} %bitcast.139, f32[16384,4]{0,1:T(4,128)S(1)} %copy-done.8, f32[16384,4,64]{0,2,1:T(8,128)} %bitcast.137, f32[16384,4]{0,1:T(4,128)S(1)} %copy-done.6), kind=kLoop, calls=%fused_computation.8 | loop fusion | flops 14680064 | bytes 42467328 | tf_op jit(solution)/shard_map/reduce_sum | solution.py:73
  596.1 7.0 copy.39
  603.1 7.9 %add.971 = f32[128,1,8192]{2,0,1:T(8,128)} reshape(f32[16384,64]{1,0:T(8,128)} %copy.39) | data formatting | bytes 8388608 | tf_op jit(solution)/shard_map/add | solution.py:73
  628.5 29.7 %all-to-all-done.3 = bf16[128,2,4096]{2,1,0:T(2,128)(2,1)S(1)} async-done(((bf16[128,2,4096]{2,1,0:T(2,128)(2,1)}), bf16[128,2,4096]{2,1,0:T(2,128)(2,1)S(1)}, u32[]{:S(2)}, u32[]{:S(2)}) %all-to-all-start.3) | async-done | bytes 2097184 | tf_op jit(solution)/shard_map/all_to_all | solution.py:148
  658.2 6.8 reshape.1163
  665.0 12.6 %reduce.17 = bf16[128,8192]{1,0:T(8,128)(2,1)S(1)} reduce(bf16[128,1,8192]{2,1,0:T(2,128)(2,1)} %reshape.1163, bf16[]{:T(256)} %constant.99), dimensions={1}, to_apply=%all_to_all.28.reduce_sub_computation | reduce | bytes 4194306 | tf_op jit(solution)/shard_map/all_to_all | solution.py:148
  683.1 24.7 %gather_fusion.4 = bf16[8192,64]{1,0:T(8,128)(2,1)S(1)} fusion(bf16[16384,64]{1,0:T(8,128)(2,1)} %reshape_reshape.4, s32[8192]{0:T(1024)S(1)} %broadcast_clamp_fusion.4), kind=kCustom, calls=%fused_computation.4 | custom fusion | bytes 2129920 | tf_op jit(solution)/shard_map/gather | solution.py:152
  (156 shorter events, 121.5 us)
Async XLA Ops:
  0.0 206.7 %copy-start = (bf16[1,512,256]{2,1,0:T(8,128)(2,1)S(1)}, bf16[1,512,256]{2,1,0:T(8,128)(2,1)}, u32[]{:S(2)}) copy-start(bf16[1,512,256]{2,1,0:T(8,128)(2,1)} %param.13) | copy-start | bytes 786436
  0.0 50.5 %copy-start.14 = (bf16[1,7,7,256]{3,2,1,0:T(8,128)(2,1)S(1)}, bf16[1,7,7,256]{3,2,1,0:T(8,128)(2,1)}, u32[]{:S(2)}) copy-start(bf16[1,7,7,256]{3,2,1,0:T(8,128)(2,1)} %param.10) | copy-start | bytes 75268
  0.0 52.3 %copy-start.12 = (f32[2,8192]{1,0:T(2,128)S(1)}, f32[2,8192]{1,0:T(2,128)}, u32[]{:S(2)}) copy-start(f32[2,8192]{1,0:T(2,128)} %param.17) | copy-start | bytes 196612
  1.8 150.8 %collective-permute-start = (bf16[3,90,256]{2,1,0:T(8,128)(2,1)}, bf16[3,90,256]{2,1,0:T(8,128)(2,1)S(1)}, u32[]{:S(2)}, u32[]{:S(2)}) collective-permute-start(bf16[3,90,256]{2,1,0:T(8,128)(2,1)} %get-tuple-element.30), channel_id=1, source_target_pairs={{0,16},{16,32},{32,48},{48,64},{64,80},{80,96},{96,112},{112,0},{1... | collective-permute-start | bytes 414728 | tf_op jit(solution)/shard_map/ppermute | solution.py:14
  4.8 147.9 %collective-permute-start.1 = (bf16[3,90,256]{2,1,0:T(8,128)(2,1)}, bf16[3,90,256]{2,1,0:T(8,128)(2,1)S(1)}, u32[]{:S(2)}, u32[]{:S(2)}) collective-permute-start(bf16[3,90,256]{2,1,0:T(8,128)(2,1)} %get-tuple-element.29), channel_id=1, source_target_pairs={{16,0},{32,16},{48,32},{64,48},{80,64},{96,80},{112,96},{0,112},{1... | collective-permute-start | bytes 414728 | tf_op jit(solution)/shard_map/ppermute | solution.py:15
  6.4 146.2 %copy-start.3 = (bf16[45,90,256]{2,1,0:T(8,128)(2,1)S(1)}, bf16[45,90,256]{2,1,0:T(8,128)(2,1)}, u32[]{:S(2)}) copy-start(bf16[45,90,256]{2,1,0:T(8,128)(2,1)} %param.9) | copy-start | bytes 6220804
  9.0 129.9 %copy-start.10 = (s32[8192,1]{0,1:T(1,128)}, s32[8192,1]{0,1:T(1,128)S(1)}, u32[]{:S(2)}) copy-start(s32[8192,1]{0,1:T(1,128)S(1)} %compare_select_fusion.4) | copy-start | bytes 98308
  40.2 74.8 %all-to-all-start.2 = ((s32[128,1,128]{2,1,0:T(1,128)}), s32[128,1,128]{2,1,0:T(1,128)S(1)}, u32[]{:S(2)}, u32[]{:S(2)}) async-start(s32[128,1,128]{2,1,0:T(1,128)} %bitcast.73), calls=%async_computation.2 | async-start | bytes 131072 | tf_op jit(solution)/shard_map/all_to_all | solution.py:135
  115.0 19.4 %all-to-all-start.1 = ((f32[128,1,128]{2,1,0:T(1,128)}), f32[128,1,128]{2,1,0:T(1,128)S(1)}, u32[]{:S(2)}, u32[]{:S(2)}) async-start(f32[128,1,128]{2,1,0:T(1,128)} %bitcast.9), calls=%async_computation.1 | async-start | bytes 131072 | tf_op jit(solution)/shard_map/all_to_all | solution.py:145
  134.4 14.1 %all-to-all-start = ((f32[128,1,128]{2,1,0:T(1,128)}), f32[128,1,128]{2,1,0:T(1,128)S(1)}, u32[]{:S(2)}, u32[]{:S(2)}) async-start(f32[128,1,128]{2,1,0:T(1,128)} %bitcast.6), calls=%async_computation | async-start | bytes 131072 | tf_op jit(solution)/shard_map/all_to_all | solution.py:144
  148.5 11.4 %copy-start.33 = (pred[51]{0:T(512)(128)(4,1)S(1)}, pred[51]{0:T(512)(128)(4,1)}, u32[]{:S(2)}) copy-start(pred[51]{0:T(512)(128)(4,1)} %compare_and_fusion) | copy-start | bytes 157
  152.9 6.9 collective-permute-start.2
  153.3 6.6 collective-permute-start.3
  215.2 4.1 collective-permute-start.4
  217.9 3.5 collective-permute-start.5
  222.8 14.3 %collective-permute-start.6 = (bf16[49,2,64]{2,1,0:T(2,128)(2,1)S(1)}, bf16[49,2,64]{2,1,0:T(2,128)(2,1)S(1)}, u32[]{:S(2)}, u32[]{:S(2)}) collective-permute-start(bf16[49,2,64]{2,1,0:T(2,128)(2,1)S(1)} %copy.26), channel_id=1, source_target_pairs={{0,1},{1,2},{2,3},{3,4},{4,5},{5,6},{6,7},{7,8},{8,9},{9,10},{10,1... | collective-permute-start | bytes 37640 | tf_op jit(solution)/shard_map/ppermute | solution.py:14
  223.6 14.1 %collective-permute-start.7 = (bf16[49,2,64]{2,1,0:T(2,128)(2,1)S(1)}, bf16[49,2,64]{2,1,0:T(2,128)(2,1)S(1)}, u32[]{:S(2)}, u32[]{:S(2)}) collective-permute-start(bf16[49,2,64]{2,1,0:T(2,128)(2,1)S(1)} %copy.27), channel_id=1, source_target_pairs={{1,0},{2,1},{3,2},{4,3},{5,4},{6,5},{7,6},{8,7},{9,8},{10,9},{11,1... | collective-permute-start | bytes 37640 | tf_op jit(solution)/shard_map/ppermute | solution.py:15
  551.5 12.4 %copy-start.5 = (f32[16384,4]{0,1:T(4,128)S(1)}, f32[16384,4]{0,1:T(4,128)}, u32[]{:S(2)}) copy-start(f32[16384,4]{0,1:T(4,128)} %pad_maximum_fusion.2) | copy-start | bytes 786436
  551.5 12.4 %copy-start.7 = (f32[16384,4]{0,1:T(4,128)S(1)}, f32[16384,4]{0,1:T(4,128)}, u32[]{:S(2)}) copy-start(f32[16384,4]{0,1:T(4,128)} %pad_maximum_fusion.3) | copy-start | bytes 786436
  563.9 12.5 %copy-start.6 = (f32[16384,4]{0,1:T(4,128)S(1)}, f32[16384,4]{0,1:T(4,128)}, u32[]{:S(2)}) copy-start(f32[16384,4]{0,1:T(4,128)} %pad_maximum_fusion.4) | copy-start | bytes 786436
  563.9 12.5 %copy-start.8 = (f32[16384,4]{0,1:T(4,128)S(1)}, f32[16384,4]{0,1:T(4,128)}, u32[]{:S(2)}) copy-start(f32[16384,4]{0,1:T(4,128)} %pad_maximum_fusion.5) | copy-start | bytes 786436
  618.5 10.0 %copy-start.11 = (s32[8192,1]{0,1:T(1,128)S(1)}, s32[8192,1]{0,1:T(1,128)}, u32[]{:S(2)}) copy-start(s32[8192,1]{0,1:T(1,128)} %copy-done.10) | copy-start | bytes 98308
  623.0 35.2 %all-to-all-start.3 = ((bf16[128,2,4096]{2,1,0:T(2,128)(2,1)}), bf16[128,2,4096]{2,1,0:T(2,128)(2,1)S(1)}, u32[]{:S(2)}, u32[]{:S(2)}) async-start(bf16[128,2,4096]{2,1,0:T(2,128)(2,1)} %reshape.1162), calls=%async_computation.3 | async-start | bytes 4194304 | tf_op jit(solution)/shard_map/all_to_all | solution.py:148
  683.1 26.3 %copy-start.1 = (bf16[1,512,256]{2,1,0:T(8,128)(2,1)S(1)}, bf16[1,512,256]{2,1,0:T(8,128)(2,1)}, u32[]{:S(2)}) copy-start(bf16[1,512,256]{2,1,0:T(8,128)(2,1)} %param.13) | copy-start | bytes 786436
  (24 other events, 90.7 us)
where the time goes:
time: 719 us; the launch traced here: 710 us
  local copies, waits for them, and re-layouts  497 us (69%)
  other arithmetic  102 us (14%)
  waiting for transfers between devices  51.5 us (7%)
  starting transfers between devices  46.6 us (6%)
  matrix products  10.8 us (2%)
    gather x4, local copies, waits for them, and re-layouts, read_cells(): gathered = windowed[position].reshape(count, 4, width)  261 us
    convert_element_type x4, local copies, waits for them, and re-layouts, read_cells(): gathered.astype(jnp.float32)  49.3 us
    scatter x1, local copies, waits for them, and re-layouts, shards(): offset_buffer = jnp.zeros((devices * capacity,), jnp.int32).at[destinatio...  31.2 us
    scatter x1, local copies, waits for them, and re-layouts, shards(): rowfrac_buffer = jnp.zeros((devices * capacity,), jnp.float32).at[destina...  31 us
    scatter x1, local copies, waits for them, and re-layouts, shards(): colfrac_buffer = jnp.zeros((devices * capacity,), jnp.float32).at[destina...  31 us
    reduce_sum x1, other arithmetic, conv_block(): centre_mean = jnp.mean(summed, axis=-1, keepdims=True)  30 us
    all_to_all x1, waiting for transfers between devices, shards(): lax.all_to_all(values.reshape(values.shape[0], -1), ('lat', 'lon'), split...  29.7 us
    reduce_sum x2, other arithmetic, read_cells(): jnp.sum(weight[:, :, None] * gathered.astype(jnp.float32), axis=1)  27.3 us
  transfers between devices with their start and end apart: 12, of which 6 were waited for; matrix products, arithmetic and copies ran while one was open for 16% of the time, Pallas kernels for 0%

commit v1 on v0

v1 whole, which is shorter than its diff:
```python
import functools
import jax, jax.numpy as jnp
from jax import lax
from jax.experimental import pallas as pl
from jax.experimental.pallas import tpu as pltpu
from jax.sharding import PartitionSpec as P
F32, BF16, I32 = jnp.float32, jnp.bfloat16, jnp.int32
VM = pltpu.VMEM


def route_kernel(owner_ref, off_ref, fr_ref, req_ref, row_ref, half_ref, hot_ref, val_ref):
    blocks = owner_ref.shape[0]
    sub = lax.broadcasted_iota(I32, (128, 128), 0)
    lane = lax.broadcasted_iota(I32, (128, 128), 1)
    upper = jnp.where(sub < lane, 1.0, 0.0).astype(BF16)
    prefix = jnp.concatenate([upper, jnp.ones((128, 128), BF16)], axis=1)
    group = 8

    def step(k, base):
        for u in range(group):
            b = k * group + u
            mine = owner_ref[pl.ds(b, 1), :]
            hot = jnp.where(mine == sub, 1.0, 0.0)
            hot16 = hot.astype(BF16)
            hot_ref[:, u * 128:(u + 1) * 128] = hot16
            sums = jnp.dot(hot16, prefix, preferred_element_type=F32)
            ranks = jnp.sum((sums[:, :128] + base) * hot, axis=0, keepdims=True)
            base = base + sums[:, 128:]
            rank = ranks.astype(I32)
            row_ref[pl.ds(b, 1), :] = mine * 64 + (rank & 63)
            half_ref[pl.ds(b, 1), :] = rank >> 6
            there = rank == sub
            off = off_ref[pl.ds(b, 1), :]
            fy = fr_ref[0:1, pl.ds(pl.multiple_of(b * 128, 128), 128)]
            fx = fr_ref[1:2, pl.ds(pl.multiple_of(b * 128, 128), 128)]
            fy_hi = fy.astype(BF16).astype(F32)
            fx_hi = fx.astype(BF16).astype(F32)
            parts = [(off >> 6).astype(F32), (off & 63).astype(F32), fy_hi, fy - fy_hi, fx_hi, fx - fx_hi]
            for p, part in enumerate(parts):
                val_ref[p * 128:(p + 1) * 128, u * 128:(u + 1) * 128] = jnp.where(there, part, 0.0).astype(BF16)
        acc = lax.dot_general(hot_ref[...], val_ref[...], (((1,), (1,)), ((), ())), preferred_element_type=F32)
        new = jnp.concatenate(
            [acc[:, 0:128] * 64.0 + acc[:, 128:256], acc[:, 256:384] + acc[:, 384:512], acc[:, 512:640] + acc[:, 640:768]],
            axis=1)
        req_ref[...] = jnp.where(k == 0, new, req_ref[...] + new)
        return base

    lax.fori_loop(0, blocks // group, step, jnp.zeros((128, 128), F32))


def route(owner, offsets, fractions):
    n = owner.shape[0]
    return pl.pallas_call(
        route_kernel,
        out_shape=[jax.ShapeDtypeStruct((128, 384), F32), jax.ShapeDtypeStruct((n // 128, 128), I32), jax.ShapeDtypeStruct((n // 128, 128), I32)],
        in_specs=[pl.BlockSpec(memory_space=VM)] * 3,
        out_specs=[pl.BlockSpec(memory_space=VM)] * 3,
        scratch_shapes=[VM((128, 1024), BF16), VM((768, 1024), BF16)],
        compiler_params=pltpu.CompilerParams(vmem_limit_bytes=32 << 20),
        name="route",
    )(owner.reshape(n // 128, 128), offsets.reshape(n // 128, 128), fractions)


def gather_kernel(idx_ref, fr_ref, table_ref, out_ref, g0_ref, g1_ref):
    lane = lax.broadcasted_iota(I32, (8, 128), 1)
    low = lane < 64
    one = jnp.where(low, -1.0, 0.0)
    two = jnp.where(low, 1.0, 2.0)
    one_c, two_c = -0.5 * one * one, -0.5 * two * two
    sources = out_ref.shape[0] // 64

    def fetch(d, g_ref):
        for s in range(128):
            at = pl.multiple_of(idx_ref[d, s], 8)
            g_ref[s * 8:(s + 1) * 8, :] = table_ref[pl.ds(at, 8), :]

    def work(d, g_ref):
        rows = fr_ref[pl.ds(d, 1), :]
        cy = jnp.transpose(jnp.broadcast_to(rows[:, 128:256], (128, 128)))
        cx = jnp.transpose(jnp.broadcast_to(rows[:, 256:384], (128, 128)))

        def part(g):
            fy = cy[g * 8:(g + 1) * 8, :]
            fx = cx[g * 8:(g + 1) * 8, :]
            am = jnp.exp(-fy - 0.5)
            a1 = jnp.exp(fy - 0.5)
            a2 = jnp.exp(fy + fy - 2.0)
            b0 = jnp.exp(fx * one + one_c)
            b1 = jnp.exp(fx * two + two_c)
            v = [g_ref[pl.ds(g * 64 + s, 8, stride=8), :] for s in range(8)]
            m = [v[2 * i] * b0 + v[2 * i + 1] * b1 for i in range(4)]
            tot = m[0] * am + m[1] + m[2] * a1 + m[3] * a2
            bs = b0 + b1
            bs = bs + pltpu.roll(bs, 64, 1)
            return tot / (bs * (am + 1.0 + a1 + a2))

        for g in range(0, 8, 2):
            res = []
            for q in (g, g + 1):
                p0, p1 = part(q), part(q + 8)
                res.append(jnp.where(low, p0, p1) + pltpu.roll(jnp.where(low, p1, p0), 64, 1))
            out_ref[pl.ds(pl.multiple_of(d * 64 + g * 8, 16), 16), :] = jnp.concatenate(res, axis=0).astype(BF16)

    fetch(0, g0_ref)

    def step(k, _):
        d = k * 2
        fetch(d + 1, g1_ref)
        work(d, g0_ref)
        fetch(jnp.minimum(d + 2, sources - 1), g0_ref)
        work(d + 1, g1_ref)
        return 0

    lax.fori_loop(0, sources // 2, step, 0)


def gather(idx, req, table):
    return pl.pallas_call(
        gather_kernel,
        out_shape=jax.ShapeDtypeStruct((128 * 64, 128), BF16),
        in_specs=[pl.BlockSpec(memory_space=pltpu.SMEM), pl.BlockSpec(memory_space=VM), pl.BlockSpec(memory_space=VM)],
        out_specs=pl.BlockSpec(memory_space=VM),
        scratch_shapes=[VM((1024, 128), F32), VM((1024, 128), F32)],
        compiler_params=pltpu.CompilerParams(vmem_limit_bytes=48 << 20),
        name="gather",
    )(idx, req, table)


def place_kernel(idx_ref, half_ref, ret_ref, out_ref, wide_ref, x0_ref, x1_ref):
    rows = ret_ref.shape[0]

    def widen(k, _):
        at = pl.multiple_of(k * 256, 256)
        wide_ref[pl.ds(at, 256), :] = ret_ref[pl.ds(at, 256), :].astype(F32)
        return 0

    lax.fori_loop(0, rows // 256, widen, 0)

    def fetch(k, x_ref):
        for t in range(128):
            x_ref[t:t + 1, :] = wide_ref[pl.ds(idx_ref[k, t], 1), :]

    def work(k, x_ref):
        y = jnp.transpose(x_ref[...])
        second = half_ref[pl.ds(k, 1), :] > 0
        out_ref[:, pl.ds(pl.multiple_of(k * 128, 128), 128)] = jnp.where(second, y[64:], y[:64]).astype(BF16)

    blocks = half_ref.shape[0]
    fetch(0, x0_ref)

    def step(j, _):
        k = j * 2
        fetch(k + 1, x1_ref)
        work(k, x0_ref)
        fetch(jnp.minimum(k + 2, blocks - 1), x0_ref)
        work(k + 1, x1_ref)
        return 0

    lax.fori_loop(0, blocks // 2, step, 0)


def place(idx, half, ret):
    n = half.shape[0] * 128
    return pl.pallas_call(
        place_kernel,
        out_shape=jax.ShapeDtypeStruct((64, n), BF16),
        in_specs=[pl.BlockSpec(memory_space=pltpu.SMEM), pl.BlockSpec(memory_space=VM), pl.BlockSpec(memory_space=VM)],
        out_specs=pl.BlockSpec(memory_space=VM),
        scratch_shapes=[VM(ret.shape, F32), VM((128, 128), F32), VM((128, 128), F32)],
        compiler_params=pltpu.CompilerParams(vmem_limit_bytes=32 << 20),
        name="place",
    )(idx, half, ret)


COLS, EXT = 96, 104


def grid_kernel(ext_ref, tap_ref, gain_ref, up_ref, down_ref, read_ref, out_ref, x_ref, tap8_ref, mix_ref, *, total_rows, tile_rows):
    first = lax.axis_index("lat") * tile_rows - 1
    for h in range(2):
        for t in range(49):
            tap8_ref[h, t * 8:(t + 1) * 8, :] = jnp.broadcast_to(tap_ref[t:t + 1, h * 128:(h + 1) * 128].astype(F32), (8, 128))

    def relay(r, _):
        for s in range(8):
            row = ext_ref[6 * s + r].astype(F32)
            for h in range(2):
                for c in range(EXT // 8):
                    x_ref[h, pl.ds((r * EXT + c * 8) * 8 + s, 8, stride=8), :] = row[c * 8:(c + 1) * 8, h * 128:(h + 1) * 128]
        return 0

    lax.fori_loop(0, 12, relay, 0)

    for h in range(2):
        def conv(c, _):
            acc = [None] * 6
            for b in range(7):
                x = [x_ref[h, pl.ds(pl.multiple_of((rr * EXT + c + b) * 8, 8), 8), :] for rr in range(12)]
                for a in range(7):
                    t = a * 7 + b
                    k = tap8_ref[h, t * 8:(t + 1) * 8, :]
                    for r in range(6):
                        p = x[r + a] * k
                        acc[r] = p if acc[r] is None else acc[r] + p
            for r in range(6):
                mix_ref[pl.ds(pl.multiple_of((r * COLS + c) * 8, 8), 8), h * 128:(h + 1) * 128] = acc[r]
            return 0

        lax.fori_loop(0, COLS, conv, 0)

    n = COLS * 8
    low = lax.broadcasted_iota(I32, (n, 128), 1) < 64
    strip = lax.broadcasted_iota(I32, (n, 128), 0) & 7

    def mlp(r, _):
        at = pl.multiple_of(r * n, n)
        m = mix_ref[pl.ds(at, n), :]
        m = m - jnp.mean(m, axis=1, keepdims=True)
        var = jnp.mean(m * m, axis=1, keepdims=True)
        normed = (m * lax.rsqrt(var + 1e-6) * gain_ref[...]).astype(BF16)
        hidden = jax.nn.gelu(jnp.dot(normed, up_ref[...], preferred_element_type=F32)).astype(BF16)
        delta = jnp.dot(hidden, down_ref[...], preferred_element_type=F32)
        mid = pl.multiple_of(((r + 3) * EXT + 3) * 8, 8)
        centre = jnp.concatenate([x_ref[0, pl.ds(mid, n), :], x_ref[1, pl.ds(mid, n), :]], axis=1)
        field = (centre + delta).astype(BF16)
        p = lax.dot_general(field, read_ref[...], (((1,), (1,)), ((), ())), preferred_element_type=F32)
        p = p.astype(BF16).astype(F32)
        row = first + strip * 6 + r
        p = jnp.where((row >= 0) & (row < total_rows), p, 0.0)
        out_ref[pl.ds(at, n), :] = jnp.where(low, p, jnp.concatenate([p[8:], p[:8]], axis=0))
        return 0

    lax.fori_loop(0, 6, mlp, 0)


def grid_block(ext, taps, gain, up, down, read2, total_rows, tile_rows):
    return pl.pallas_call(
        functools.partial(grid_kernel, total_rows=total_rows, tile_rows=tile_rows),
        out_shape=jax.ShapeDtypeStruct((6 * COLS * 8, 128), F32),
        in_specs=[pl.BlockSpec(memory_space=VM)] * 6,
        out_specs=pl.BlockSpec(memory_space=VM),
        scratch_shapes=[VM((2, 12 * EXT * 8, 128), F32), VM((2, 49 * 8, 128), F32), VM((6 * COLS * 8, 256), F32)],
        compiler_params=pltpu.CompilerParams(vmem_limit_bytes=48 << 20),
        name="grid_block",
    )(ext, taps, gain, up, down, read2)


def gather2_kernel(idx_ref, fr_ref, q_ref, out_ref, table_ref, g0_ref, g1_ref, *, tile_cols):
    def build(c, _):
        for r in range(6):
            for jj in range(2):
                q = q_ref[pl.ds(pl.multiple_of((r * COLS + c + 2 * jj) * 8, 8), 8), :]
                for i in range(4):
                    table_ref[pl.ds(((r - i + 3) * tile_cols + c) * 8 + 2 * i + jj, 8, stride=6 * tile_cols * 8), :] = q
        return 0

    lax.fori_loop(0, tile_cols, build, 0)
    gather_kernel(idx_ref, fr_ref, table_ref, out_ref, g0_ref, g1_ref)


def gather2(idx, req, q, tile_cols=90):
    return pl.pallas_call(
        functools.partial(gather2_kernel, tile_cols=tile_cols),
        out_shape=jax.ShapeDtypeStruct((128 * 64, 128), BF16),
        in_specs=[pl.BlockSpec(memory_space=pltpu.SMEM), pl.BlockSpec(memory_space=VM), pl.BlockSpec(memory_space=VM)],
        out_specs=pl.BlockSpec(memory_space=VM),
        scratch_shapes=[VM((51 * tile_cols * 8, 128), F32), VM((1024, 128), F32), VM((1024, 128), F32)],
        compiler_params=pltpu.CompilerParams(vmem_limit_bytes=48 << 20),
        name="gather",
    )(idx, req, q)


def shift(x, d_lat, d_lon):
    n_lat, n_lon = lax.axis_size("lat"), lax.axis_size("lon")
    pairs = []
    for p in range(n_lat):
        for q in range(n_lon):
            if 0 <= p + d_lat < n_lat:
                pairs.append((p * n_lon + q, (p + d_lat) * n_lon + (q + d_lon) % n_lon))
    return lax.ppermute(x, ("lat", "lon"), pairs)


def extended(grid):
    rows, cols = grid.shape[:2]
    top, bottom = grid[rows - 4:], grid[:5]
    parts = [
        [shift(top[:, cols - 4:], 1, 1), shift(top, 1, 0), shift(top[:, :5], 1, -1)],
        [shift(grid[:, cols - 4:], 0, 1), grid, shift(grid[:, :5], 0, -1)],
        [shift(bottom[:, cols - 4:], -1, 1), shift(bottom, -1, 0), shift(bottom[:, :5], -1, -1)],
    ]
    full = jnp.concatenate([jnp.concatenate(p, axis=1) for p in parts], axis=0)
    return jnp.pad(full, ((0, 0), (0, EXT - cols - 9), (0, 0)))


def shards(grid, dw_kernel, norm_gain, w_up, w_down, w_read, owner, offsets, fractions):
    tile_rows, tile_cols = grid.shape[:2]
    req, row, half = route(owner, offsets, fractions)
    ext = extended(grid)
    req = lax.all_to_all(req, ("lat", "lon"), split_axis=0, concat_axis=0, tiled=True)
    idx = (req[:, :128].astype(I32) + 3 * tile_cols) * 8
    read = w_read.T
    q = grid_block(
        ext, dw_kernel.reshape(49, -1), norm_gain, w_up[0], w_down[0], jnp.concatenate([read, read], axis=0),
        tile_rows * lax.axis_size("lat"), tile_rows)
    out = gather2(idx, req, q, tile_cols)
    ret = lax.all_to_all(out, ("lat", "lon"), split_axis=0, concat_axis=0, tiled=True)
    return place(row, half, ret).T


def solution(mesh):
    return jax.shard_map(
        shards,
        mesh=mesh,
        in_specs=(P("lat", "lon", None), P(), P(), P(), P(), P(), P(("lat", "lon"), None), P(("lat", "lon")), P(None, ("lat", "lon"))),
        out_specs=P(("lat", "lon"), None),
        check_vma=False,
    )
```

time: 719 us -> 202 us (0.28); the launches traced: 710 us -> 201 us
  local copies, waits for them, and re-layouts: 497 us -> 13.4 us
  Pallas kernels: 0 us -> 99.9 us
  other arithmetic: 102 us -> 8.15 us
  waiting for transfers between devices: 51.5 us -> 2.53 us
  blocking collectives: 0 us -> 37.7 us
  matrix products: 10.8 us -> 0 us
  starting transfers between devices: 46.6 us -> 38.7 us
    gather x6 -> x0, local copies, waits for them, and re-layouts: 287 us -> none  [the longest x4 261 us: read_cells(): gathered = windowed[position].reshape(count, 4, width)]
    pallas_call x0 -> x4, Pallas kernels: none -> 99.9 us  [the longest x1 48 us: gather2(): pl.pallas_call(functools.partial(gather2_kernel, tile_cols=tile_cols), ou...]
    scatter x3 -> x0, local copies, waits for them, and re-layouts: 93.3 us -> none  [the longest x1 31.2 us: shards(): offset_buffer = jnp.zeros((devices * capacity,), jnp.int32).at[destinatio...]
    reduce_sum x5 -> x0, other arithmetic: 62.3 us -> none  [the longest x1 30 us: conv_block(): centre_mean = jnp.mean(summed, axis=-1, keepdims=True)]
    convert_element_type x5 -> x0, local copies, waits for them, and re-layouts: 49.8 us -> none  [the longest x4 49.3 us: read_cells(): gathered.astype(jnp.float32)]
    all_to_all x4 -> x1, waiting for transfers between devices: 47.8 us -> 0.01 us  [shards(): lax.all_to_all(req, ('lat', 'lon'), split_axis=0, concat_axis=0, tiled=True)]
    all_to_all x0 -> x1, blocking collectives: none -> 37.7 us  [shards(): lax.all_to_all(out, ('lat', 'lon'), split_axis=0, concat_axis=0, tiled=True)]
    all_to_all x4 -> x1, starting transfers between devices: 29.9 us -> 11.5 us  [shards(): lax.all_to_all(req, ('lat', 'lon'), split_axis=0, concat_axis=0, tiled=True)]
  transfers between devices with their start and end apart: 12 -> 9, of which waited for: 6 -> 1; matrix products, arithmetic and copies ran while one was open for 16% -> 5% of each run, Pallas kernels for 0% -> 0%
where the time goes in v1:
time: 202 us; the launch traced here: 201 us
  Pallas kernels  99.9 us (49%)
  starting transfers between devices  38.7 us (19%)
  blocking collectives  37.7 us (19%)
  local copies, waits for them, and re-layouts  13.4 us (7%)
  other arithmetic  8.15 us (4%)
  waiting for transfers between devices  2.53 us (1%)
    pallas_call x1, Pallas kernels, gather2(): pl.pallas_call(functools.partial(gather2_kernel, tile_cols=tile_cols), ou...  48 us
    all_to_all x1, blocking collectives, shards(): lax.all_to_all(out, ('lat', 'lon'), split_axis=0, concat_axis=0, tiled=True)  37.7 us
    pallas_call x1, Pallas kernels, grid_block(): pl.pallas_call(functools.partial(grid_kernel, total_rows=total_rows, tile...  33.2 us
    ppermute x8, starting transfers between devices, shift(): return lax.ppermute(x, ('lat', 'lon'), pairs)  27.2 us
    all_to_all x1, starting transfers between devices, shards(): lax.all_to_all(req, ('lat', 'lon'), split_axis=0, concat_axis=0, tiled=True)  11.5 us
    pallas_call x1, Pallas kernels, place(): pl.pallas_call(place_kernel, out_shape=jax.ShapeDtypeStruct((64, n), BF16...  9.97 us
    pallas_call x1, Pallas kernels, route(): pl.pallas_call(route_kernel, out_shape=[jax.ShapeDtypeStruct((128, 384),...  8.74 us
    concatenate x1, other arithmetic, extended(): full = jnp.concatenate([jnp.concatenate(p, axis=1) for p in parts], axis=0)  7.3 us
  transfers between devices with their start and end apart: 9, of which 1 were waited for; matrix products, arithmetic and copies ran while one was open for 5% of the time, Pallas kernels for 0%

profile of v1, /device:TPU:1, one launch (start us, length us, event | category | flops | bytes accessed | tf_op | source)
XLA Modules:
  0.0 200.5 jit_solution(15393578723362994)
XLA Ops:
  2.4 8.7 %route.1 = (f32[128,384]{1,0:T(8,128)S(1)}, s32[64,128]{1,0:T(8,128)S(1)}, s32[64,128]{1,0:T(8,128)S(1)}) custom-call(s32[64,128]{1,0:T(8,128)S(1)} %bitcast.19, s32[64,128]{1,0:T(8,128)S(1)} %bitcast.20, f32[2,8192]{1,0:T(2,128)S(1)} %copy-done.2), custom_call_target="tpu_custom_call" | custom-call | tf_op jit(solution)/shard_map/route/pallas_call | solution.py:53
  11.1 0.9 copy.10
  12.0 11.5 %all-to-all-start = ((f32[128,1,384]{2,1,0:T(1,128)}), f32[128,1,384]{2,1,0:T(1,128)S(1)}, u32[]{:S(2)}, u32[]{:S(2)}) async-start(f32[128,1,384]{2,1,0:T(1,128)} %copy.10), calls=%async_computation | async-start | bytes 393216 | tf_op jit(solution)/shard_map/all_to_all | solution.py:299
  23.5 1.4 slice.32
  24.9 4.6 %collective-permute-start = (bf16[4,4,256]{2,1,0:T(4,128)(2,1)}, bf16[4,4,256]{2,1,0:T(4,128)(2,1)}, u32[]{:S(2)}, u32[]{:S(2)}) collective-permute-start(bf16[4,4,256]{2,1,0:T(4,128)(2,1)} %slice.32), channel_id=1, source_target_pairs={{0,17},{1,18},{2,19},{3,20},{4,21},{5,22},{6,23},{7,24},{8,25},{9,... | collective-permute-start | bytes 24584 | tf_op jit(solution)/shard_map/ppermute | solution.py:280
  29.4 1.4 slice.37
  30.8 2.7 %collective-permute-start.5 = (bf16[5,4,256]{2,1,0:T(4,128)(2,1)}, bf16[5,4,256]{2,1,0:T(4,128)(2,1)}, u32[]{:S(2)}, u32[]{:S(2)}) collective-permute-start(bf16[5,4,256]{2,1,0:T(4,128)(2,1)} %slice.37), channel_id=1, source_target_pairs={{16,1},{17,2},{18,3},{19,4},{20,5},{21,6},{22,7},{23,8},{24,9},{25... | collective-permute-start | bytes 30728 | tf_op jit(solution)/shard_map/ppermute | solution.py:280
  33.5 1.3 slice.34
  34.8 7.1 %collective-permute-start.2 = (bf16[4,5,256]{2,1,0:T(8,128)(2,1)}, bf16[4,5,256]{2,1,0:T(8,128)(2,1)}, u32[]{:S(2)}, u32[]{:S(2)}) collective-permute-start(bf16[4,5,256]{2,1,0:T(8,128)(2,1)} %slice.34), channel_id=1, source_target_pairs={{0,31},{1,16},{2,17},{3,18},{4,19},{5,20},{6,21},{7,22},{8,23},{9,... | collective-permute-start | bytes 30728 | tf_op jit(solution)/shard_map/ppermute | solution.py:280
  41.9 1.3 slice.39
  43.2 1.9 collective-permute-start.7
  45.2 1.0 slice.38
  46.1 1.9 collective-permute-start.6
  48.9 1.1 slice.35
  50.0 0.9 slice.36
  50.9 0.9 slice.33
  53.5 4.1 %collective-permute-start.4 = (bf16[45,5,256]{2,1,0:T(8,128)(2,1)S(1)}, bf16[45,5,256]{2,1,0:T(8,128)(2,1)S(1)}, u32[]{:S(2)}, u32[]{:S(2)}) collective-permute-start(bf16[45,5,256]{2,1,0:T(8,128)(2,1)S(1)} %slice.36), channel_id=1, source_target_pairs={{0,15},{1,0},{2,1},{3,2},{4,3},{5,4},{6,5},{7,6},{8,7},{9,8},{10,9... | collective-permute-start | bytes 345608 | tf_op jit(solution)/shard_map/ppermute | solution.py:280
  57.5 4.2 %collective-permute-start.1 = (bf16[4,90,256]{2,1,0:T(8,128)(2,1)S(1)}, bf16[4,90,256]{2,1,0:T(8,128)(2,1)S(1)}, u32[]{:S(2)}, u32[]{:S(2)}) collective-permute-start(bf16[4,90,256]{2,1,0:T(8,128)(2,1)S(1)} %slice.33), channel_id=1, source_target_pairs={{0,16},{1,17},{2,18},{3,19},{4,20},{5,21},{6,22},{7,23},{8,24},{9,... | collective-permute-start | bytes 552968 | tf_op jit(solution)/shard_map/ppermute | solution.py:280
  61.8 2.5 %collective-permute-done.1 = bf16[4,90,256]{2,1,0:T(8,128)(2,1)S(1)} collective-permute-done((bf16[4,90,256]{2,1,0:T(8,128)(2,1)S(1)}, bf16[4,90,256]{2,1,0:T(8,128)(2,1)S(1)}, u32[]{:S(2)}, u32[]{:S(2)}) %collective-permute-start.1) | collective-permute-done | bytes 184352 | tf_op jit(solution)/shard_map/ppermute | solution.py:280
  64.3 7.3 %fusion.12.ext_ref = bf16[54,104,256]{2,1,0:T(8,128)(2,1)S(1)} fusion(bf16[5,5,256]{2,1,0:T(8,128)(2,1)S(1)} %collective-permute-done.7, bf16[5,90,256]{2,1,0:T(8,128)(2,1)S(1)} %collective-permute-done.6, bf16[5,4,256]{2,1,0:T(4,128)(2,1)} %collective-permute-done.5, bf16[45,5,256]{2,1,0:T(8,128)(2,1)S(1)} %collective-permute-done.4, ...), kind=kLoop, calls=%fused_computation.13 | loop fusion | flops 40255488 | bytes 5612544 | tf_op jit(solution)/shard_map/concatenate | solution.py:291
  71.7 33.2 %grid_block.1.q_ref = f32[4608,128]{1,0:T(8,128)S(1)} custom-call(bf16[54,104,256]{2,1,0:T(8,128)(2,1)S(1)} %fusion.12.ext_ref, bf16[49,256]{1,0:T(8,128)(2,1)S(1)} %reshape.15.tap_ref, f32[1,256]{1,0:T(1,128)S(1)} %copy-done.5, bf16[256,512]{1,0:T(8,128)(2,1)S(1)} %bitcast.16, bf16[512,256]{1,0:T(8,128)(2,1)S(1)} %bitcast.17, ...), custom_call_target="tpu_custom_call" | custom-call | tf_op jit(solution)/shard_map/grid_block/pallas_call | solution.py:237
  104.9 48.0 %gather.1 = bf16[8192,128]{1,0:T(8,128)(2,1)S(1)} custom-call(s32[128,128]{1,0:T(8,128)S(1)} %fusion.18.idx_ref, f32[128,384]{1,0:T(8,128)S(1)} %bitcast.15, f32[4608,128]{1,0:T(8,128)S(1)} %grid_block.1.q_ref), custom_call_target="tpu_custom_call" | custom-call | tf_op jit(solution)/shard_map/gather/pallas_call | solution.py:262
  152.9 37.7 %all_to_all.22 = bf16[128,64,128]{2,1,0:T(8,128)(2,1)S(1)} all-to-all(bf16[128,64,128]{2,1,0:T(8,128)(2,1)S(1)} %bitcast.13), channel_id=1, replica_groups=mesh['lat'=8,'lon'=16] {'lat','lon'}, dimensions={0} | all-to-all | bytes 4194304 | tf_op jit(solution)/shard_map/all_to_all | solution.py:306
  190.6 10.0 %place.1 = bf16[64,8192]{1,0:T(8,128)(2,1)} custom-call(s32[64,128]{1,0:T(8,128)S(1)} %get-tuple-element.8.idx_ref, s32[64,128]{1,0:T(8,128)S(1)} %get-tuple-element.9.half_ref, bf16[8192,128]{1,0:T(8,128)(2,1)S(1)} %bitcast.12), custom_call_target="tpu_custom_call" | custom-call | tf_op jit(solution)/shard_map/place/pallas_call | solution.py:164
  (27 shorter events, 4.8 us)
Async XLA Ops:
  0.0 0.8 copy-start.2
  0.8 0.8 copy-start.3
  1.6 0.8 copy-start.4
  2.4 62.0 %copy-start.6 = (bf16[45,90,256]{2,1,0:T(8,128)(2,1)S(1)}, bf16[45,90,256]{2,1,0:T(8,128)(2,1)}, u32[]{:S(2)}) copy-start(bf16[45,90,256]{2,1,0:T(8,128)(2,1)} %param.9) | copy-start | bytes 6220804
  12.0 40.6 %all-to-all-start = ((f32[128,1,384]{2,1,0:T(1,128)}), f32[128,1,384]{2,1,0:T(1,128)S(1)}, u32[]{:S(2)}, u32[]{:S(2)}) async-start(f32[128,1,384]{2,1,0:T(1,128)} %copy.10), calls=%async_computation | async-start | bytes 393216 | tf_op jit(solution)/shard_map/all_to_all | solution.py:299
  24.9 27.8 %collective-permute-start = (bf16[4,4,256]{2,1,0:T(4,128)(2,1)}, bf16[4,4,256]{2,1,0:T(4,128)(2,1)}, u32[]{:S(2)}, u32[]{:S(2)}) collective-permute-start(bf16[4,4,256]{2,1,0:T(4,128)(2,1)} %slice.32), channel_id=1, source_target_pairs={{0,17},{1,18},{2,19},{3,20},{4,21},{5,22},{6,23},{7,24},{8,25},{9,... | collective-permute-start | bytes 24584 | tf_op jit(solution)/shard_map/ppermute | solution.py:280
  30.8 22.6 %collective-permute-start.5 = (bf16[5,4,256]{2,1,0:T(4,128)(2,1)}, bf16[5,4,256]{2,1,0:T(4,128)(2,1)}, u32[]{:S(2)}, u32[]{:S(2)}) collective-permute-start(bf16[5,4,256]{2,1,0:T(4,128)(2,1)} %slice.37), channel_id=1, source_target_pairs={{16,1},{17,2},{18,3},{19,4},{20,5},{21,6},{22,7},{23,8},{24,9},{25... | collective-permute-start | bytes 30728 | tf_op jit(solution)/shard_map/ppermute | solution.py:280
  34.8 22.7 %collective-permute-start.2 = (bf16[4,5,256]{2,1,0:T(8,128)(2,1)}, bf16[4,5,256]{2,1,0:T(8,128)(2,1)}, u32[]{:S(2)}, u32[]{:S(2)}) collective-permute-start(bf16[4,5,256]{2,1,0:T(8,128)(2,1)} %slice.34), channel_id=1, source_target_pairs={{0,31},{1,16},{2,17},{3,18},{4,19},{5,20},{6,21},{7,22},{8,23},{9,... | collective-permute-start | bytes 30728 | tf_op jit(solution)/shard_map/ppermute | solution.py:280
  43.2 18.5 %collective-permute-start.7 = (bf16[5,5,256]{2,1,0:T(8,128)(2,1)}, bf16[5,5,256]{2,1,0:T(8,128)(2,1)S(1)}, u32[]{:S(2)}, u32[]{:S(2)}) collective-permute-start(bf16[5,5,256]{2,1,0:T(8,128)(2,1)} %slice.39), channel_id=1, source_target_pairs={{16,15},{17,0},{18,1},{19,2},{20,3},{21,4},{22,5},{23,6},{24,7},{2... | collective-permute-start | bytes 38408 | tf_op jit(solution)/shard_map/ppermute | solution.py:280
  46.1 18.2 %collective-permute-start.6 = (bf16[5,90,256]{2,1,0:T(8,128)(2,1)S(1)}, bf16[5,90,256]{2,1,0:T(8,128)(2,1)S(1)}, u32[]{:S(2)}, u32[]{:S(2)}) collective-permute-start(bf16[5,90,256]{2,1,0:T(8,128)(2,1)S(1)} %slice.38), channel_id=1, source_target_pairs={{16,0},{17,1},{18,2},{19,3},{20,4},{21,5},{22,6},{23,7},{24,8},{25... | collective-permute-start | bytes 691208 | tf_op jit(solution)/shard_map/ppermute | solution.py:280
  52.7 9.1 %collective-permute-start.3 = (bf16[45,4,256]{2,1,0:T(4,128)(2,1)S(1)}, bf16[45,4,256]{2,1,0:T(4,128)(2,1)S(1)}, u32[]{:S(2)}, u32[]{:S(2)}) collective-permute-start(bf16[45,4,256]{2,1,0:T(4,128)(2,1)S(1)} %slice.35), channel_id=1, source_target_pairs={{0,1},{1,2},{2,3},{3,4},{4,5},{5,6},{6,7},{7,8},{8,9},{9,10},{10,1... | collective-permute-start | bytes 276488 | tf_op jit(solution)/shard_map/ppermute | solution.py:280
  53.5 8.4 %collective-permute-start.4 = (bf16[45,5,256]{2,1,0:T(8,128)(2,1)S(1)}, bf16[45,5,256]{2,1,0:T(8,128)(2,1)S(1)}, u32[]{:S(2)}, u32[]{:S(2)}) collective-permute-start(bf16[45,5,256]{2,1,0:T(8,128)(2,1)S(1)} %slice.36), channel_id=1, source_target_pairs={{0,15},{1,0},{2,1},{3,2},{4,3},{5,4},{6,5},{7,6},{8,7},{9,8},{10,9... | collective-permute-start | bytes 345608 | tf_op jit(solution)/shard_map/ppermute | solution.py:280
  57.5 6.8 %collective-permute-start.1 = (bf16[4,90,256]{2,1,0:T(8,128)(2,1)S(1)}, bf16[4,90,256]{2,1,0:T(8,128)(2,1)S(1)}, u32[]{:S(2)}, u32[]{:S(2)}) collective-permute-start(bf16[4,90,256]{2,1,0:T(8,128)(2,1)S(1)} %slice.33), channel_id=1, source_target_pairs={{0,16},{1,17},{2,18},{3,19},{4,20},{5,21},{6,22},{7,23},{8,24},{9,... | collective-permute-start | bytes 552968 | tf_op jit(solution)/shard_map/ppermute | solution.py:280
  61.7 9.9 %copy-start = (bf16[1,256,512]{2,1,0:T(8,128)(2,1)S(1)}, bf16[1,256,512]{2,1,0:T(8,128)(2,1)}, u32[]{:S(2)}) copy-start(bf16[1,256,512]{2,1,0:T(8,128)(2,1)} %param.12) | copy-start | bytes 786436
  61.8 9.9 %copy-start.1 = (bf16[1,512,256]{2,1,0:T(8,128)(2,1)S(1)}, bf16[1,512,256]{2,1,0:T(8,128)(2,1)}, u32[]{:S(2)}) copy-start(bf16[1,512,256]{2,1,0:T(8,128)(2,1)} %param.13) | copy-start | bytes 786436
  61.8 9.9 %copy-start.5 = (f32[1,256]{1,0:T(1,128)S(1)}, f32[1,256]{1,0:T(1,128)}, u32[]{:S(2)}) copy-start(f32[1,256]{1,0:T(1,128)} %gain_ref.1) | copy-start | bytes 3076

commit v2 on v1

--- a/solution.py
+++ b/solution.py
@@ -6,6 +6,8 @@
 from jax.sharding import PartitionSpec as P
 F32, BF16, I32 = jnp.float32, jnp.bfloat16, jnp.int32
 VM = pltpu.VMEM
+
+COLS, EXT = 96, 104
 
 
 def route_kernel(owner_ref, off_ref, fr_ref, req_ref, row_ref, half_ref, hot_ref, val_ref):
@@ -61,120 +63,6 @@
     )(owner.reshape(n // 128, 128), offsets.reshape(n // 128, 128), fractions)
 
 
-def gather_kernel(idx_ref, fr_ref, table_ref, out_ref, g0_ref, g1_ref):
-    lane = lax.broadcasted_iota(I32, (8, 128), 1)
-    low = lane < 64
-    one = jnp.where(low, -1.0, 0.0)
-    two = jnp.where(low, 1.0, 2.0)
-    one_c, two_c = -0.5 * one * one, -0.5 * two * two
-    sources = out_ref.shape[0] // 64
-
-    def fetch(d, g_ref):
-        for s in range(128):
-            at = pl.multiple_of(idx_ref[d, s], 8)
-            g_ref[s * 8:(s + 1) * 8, :] = table_ref[pl.ds(at, 8), :]
-
-    def work(d, g_ref):
-        rows = fr_ref[pl.ds(d, 1), :]
-        cy = jnp.transpose(jnp.broadcast_to(rows[:, 128:256], (128, 128)))
-        cx = jnp.transpose(jnp.broadcast_to(rows[:, 256:384], (128, 128)))
-
-        def part(g):
-            fy = cy[g * 8:(g + 1) * 8, :]
-            fx = cx[g * 8:(g + 1) * 8, :]
-            am = jnp.exp(-fy - 0.5)
-            a1 = jnp.exp(fy - 0.5)
-            a2 = jnp.exp(fy + fy - 2.0)
-            b0 = jnp.exp(fx * one + one_c)
-            b1 = jnp.exp(fx * two + two_c)
-            v = [g_ref[pl.ds(g * 64 + s, 8, stride=8), :] for s in range(8)]
-            m = [v[2 * i] * b0 + v[2 * i + 1] * b1 for i in range(4)]
-            tot = m[0] * am + m[1] + m[2] * a1 + m[3] * a2
-            bs = b0 + b1
-            bs = bs + pltpu.roll(bs, 64, 1)
-            return tot / (bs * (am + 1.0 + a1 + a2))
-
-        for g in range(0, 8, 2):
-            res = []
-            for q in (g, g + 1):
-                p0, p1 = part(q), part(q + 8)
-                res.append(jnp.where(low, p0, p1) + pltpu.roll(jnp.where(low, p1, p0), 64, 1))
-            out_ref[pl.ds(pl.multiple_of(d * 64 + g * 8, 16), 16), :] = jnp.concatenate(res, axis=0).astype(BF16)
-
-    fetch(0, g0_ref)
-
-    def step(k, _):
-        d = k * 2
-        fetch(d + 1, g1_ref)
-        work(d, g0_ref)
-        fetch(jnp.minimum(d + 2, sources - 1), g0_ref)
-        work(d + 1, g1_ref)
-        return 0
-
-    lax.fori_loop(0, sources // 2, step, 0)
-
-
-def gather(idx, req, table):
-    return pl.pallas_call(
-        gather_kernel,
-        out_shape=jax.ShapeDtypeStruct((128 * 64, 128), BF16),
-        in_specs=[pl.BlockSpec(memory_space=pltpu.SMEM), pl.BlockSpec(memory_space=VM), pl.BlockSpec(memory_space=VM)],
-        out_specs=pl.BlockSpec(memory_space=VM),
-        scratch_shapes=[VM((1024, 128), F32), VM((1024, 128), F32)],
-        compiler_params=pltpu.CompilerParams(vmem_limit_bytes=48 << 20),
-        name="gather",
-    )(idx, req, table)
-
-
-def place_kernel(idx_ref, half_ref, ret_ref, out_ref, wide_ref, x0_ref, x1_ref):
-    rows = ret_ref.shape[0]
-
-    def widen(k, _):
-        at = pl.multiple_of(k * 256, 256)
-        wide_ref[pl.ds(at, 256), :] = ret_ref[pl.ds(at, 256), :].astype(F32)
-        return 0
-
-    lax.fori_loop(0, rows // 256, widen, 0)
-
-    def fetch(k, x_ref):
-        for t in range(128):
-            x_ref[t:t + 1, :] = wide_ref[pl.ds(idx_ref[k, t], 1), :]
-
-    def work(k, x_ref):
-        y = jnp.transpose(x_ref[...])
-        second = half_ref[pl.ds(k, 1), :] > 0
-        out_ref[:, pl.ds(pl.multiple_of(k * 128, 128), 128)] = jnp.where(second, y[64:], y[:64]).astype(BF16)
-
-    blocks = half_ref.shape[0]
-    fetch(0, x0_ref)
-
-    def step(j, _):
-        k = j * 2
-        fetch(k + 1, x1_ref)
-        work(k, x0_ref)
-        fetch(jnp.minimum(k + 2, blocks - 1), x0_ref)
-        work(k + 1, x1_ref)
-        return 0
-
-    lax.fori_loop(0, blocks // 2, step, 0)
-
-
-def place(idx, half, ret):
-    n = half.shape[0] * 128
-    return pl.pallas_call(
-        place_kernel,
-        out_shape=jax.ShapeDtypeStruct((64, n), BF16),
-        in_specs=[pl.BlockSpec(memory_space=pltpu.SMEM), pl.BlockSpec(memory_space=VM), pl.BlockSpec(memory_space=VM)],
-        out_specs=pl.BlockSpec(memory_space=VM),
-        scratch_shapes=[VM(ret.shape, F32), VM((128, 128), F32), VM((128, 128), F32)],
-        compiler_params=pltpu.CompilerParams(vmem_limit_bytes=32 << 20),
-        name="place",
-    )(idx, half, ret)
-
-
-COLS, EXT = 96, 104
-
-
 def grid_kernel(ext_ref, tap_ref, gain_ref, up_ref, down_ref, read_ref, out_ref, x_ref, tap8_ref, mix_ref, *, total_rows, tile_rows):
     first = lax.axis_index("lat") * tile_rows - 1
     for h in range(2):
@@ -245,29 +133,162 @@
     )(ext, taps, gain, up, down, read2)
 
 
-def gather2_kernel(idx_ref, fr_ref, q_ref, out_ref, table_ref, g0_ref, g1_ref, *, tile_cols):
+def flat_weights(fr_ref, w_ref):
+    fy, fx = fr_ref[:, 128:256], fr_ref[:, 256:384]
+    a = [jnp.exp(-fy - 0.5), jnp.ones_like(fy), jnp.exp(fy - 0.5), jnp.exp(fy + fy - 2.0)]
+    b = [jnp.exp(-fx - 0.5), jnp.ones_like(fx), jnp.exp(fx - 0.5), jnp.exp(fx + fx - 2.0)]
+    scale = 1.0 / ((a[0] + a[1] + a[2] + a[3]) * (b[0] + b[1] + b[2] + b[3]))
+    a = [x * scale for x in a]
+    row = lax.broadcasted_iota(I32, (128, 1024), 0)
+    col = lax.broadcasted_iota(I32, (128, 1024), 1)
+    for s in range(8):
+        one = jnp.where(col == row * 8 + s, 1.0, 0.0).astype(BF16)
+        for half in range(2):
+            plane = (a[s // 2] * b[2 * (s % 2) + half]).astype(BF16)
+            part = jnp.dot(plane, one, preferred_element_type=F32)
+            w_ref[half] = part if s == 0 else w_ref[half] + part
+
+
+def build_table(q_ref, table_ref, tile_rows, tile_cols):
+    sub = lax.broadcasted_iota(I32, (8, 128), 0)
+    masks = {n: (sub & n) == 0 for n in (1, 2, 4)}
+
     def build(c, _):
+        q = [[None] * 2 for _ in range(9)]
+        for jj in range(2):
+            for r in range(6):
+                q[r][jj] = q_ref[pl.ds(pl.multiple_of((r * COLS + c + 2 * jj) * 8, 8), 8), :]
+            for r in range(3):
+                q[r + 6][jj] = pltpu.roll(q[r][jj], 7, 0)
         for r in range(6):
-            for jj in range(2):
-                q = q_ref[pl.ds(pl.multiple_of((r * COLS + c + 2 * jj) * 8, 8), 8), :]
-                for i in range(4):
-                    table_ref[pl.ds(((r - i + 3) * tile_cols + c) * 8 + 2 * i + jj, 8, stride=6 * tile_cols * 8), :] = q
+            v = [q[r + i][jj] for i in range(4) for jj in range(2)]
+            for n in (4, 2, 1):
+                new = list(v)
+                for k in range(8):
+                    if not k & n:
+                        new[k] = jnp.where(masks[n], v[k], pltpu.roll(v[k + n], n, 0))
+                        new[k + n] = jnp.where(masks[n], pltpu.roll(v[k], 8 - n, 0), v[k + n])
+                v = new
+            for k in range(8):
+                if 6 * k + r < tile_rows:
+                    table_ref[(6 * k + r) * tile_cols + c] = v[k]
         return 0
 
     lax.fori_loop(0, tile_cols, build, 0)
-    gather_kernel(idx_ref, fr_ref, table_ref, out_ref, g0_ref, g1_ref)
-
-
-def gather2(idx, req, q, tile_cols=90):
+
+
+def read_source(idx_ref, d, table_ref, w_ref, out_ref, low):
+    own = (lax.broadcasted_iota(I32, (32, 256), 1) >> 3) == lax.broadcasted_iota(I32, (32, 256), 0)
+    sums = []
+    for g in range(4):
+        patches = []
+        for s in range(32):
+            patches.append(table_ref[idx_ref[d, g * 32 + s]])
+        weights = [jnp.where(own, w_ref[h, pl.ds(d, 1), g * 256:(g + 1) * 256], 0.0) for h in range(2)]
+        sums.append(jnp.dot(
+            jnp.concatenate(weights, axis=0).astype(BF16), jnp.concatenate(patches, axis=0).astype(BF16),
+            preferred_element_type=F32))
+    for g in range(2):
+        first, second = sums[g], sums[g + 2]
+        keep = jnp.where(low, first[:32], second[32:])
+        move = jnp.where(low, second[:32], first[32:])
+        at = pl.multiple_of(d * 64 + g * 32, 32)
+        out_ref[pl.ds(at, 32), :] = (keep + pltpu.roll(move, 64, 1)).astype(BF16)
+
+
+def serve_kernel(idx_ref, fr_ref, q_ref, ret_ref, table_ref, w_ref, out_ref, send_sem, recv_sem, own_sem, *, tile_rows, tile_cols, n_lon, sources, unroll, turn):
+    low = lax.broadcasted_iota(I32, (32, 128), 1) < 64
+    flat_weights(fr_ref, w_ref)
+    build_table(q_ref, table_ref, tile_rows, tile_cols)
+    me = lax.axis_index("lat") * n_lon + lax.axis_index("lon")
+
+    def rows(d):
+        return pl.ds(pl.multiple_of(d * 64, 64), 64)
+
+    def send(d):
+        pltpu.make_async_remote_copy(
+            src_ref=out_ref.at[rows(d)], dst_ref=ret_ref.at[rows(me)], send_sem=send_sem, recv_sem=recv_sem,
+            device_id=(d // n_lon, d % n_lon), device_id_type=pl.DeviceIdType.MESH).start()
+
+    own = pltpu.make_async_copy(out_ref.at[rows(me)], ret_ref.at[rows(me)], own_sem)
+
+    def step(j, _):
+        for u in range(unroll):
+            d = (me + (j * unroll + u) * turn) % sources
+            read_source(idx_ref, d, table_ref, w_ref, out_ref, low)
+            if u:
+                send(d)
+            else:
+                pl.when(j > 0)(functools.partial(send, d))
+                pl.when(j == 0)(own.start)
+        return 0
+
+    lax.fori_loop(0, sources // unroll, step, 0)
+    own.wait()
+    most = pl.ds(0, (sources - 1) * 64)
+    pltpu.make_async_copy(out_ref.at[most], ret_ref.at[most], send_sem).wait()
+    pltpu.make_async_copy(out_ref.at[most], ret_ref.at[most], recv_sem).wait()
+
+
+def serve(idx, req, q, tile_rows, tile_cols, n_lon):
+    sources = idx.shape[0]
     return pl.pallas_call(
-        functools.partial(gather2_kernel, tile_cols=tile_cols),
-        out_shape=jax.ShapeDtypeStruct((128 * 64, 128), BF16),
+        functools.partial(serve_kernel, tile_rows=tile_rows, tile_cols=tile_cols, n_lon=n_lon, sources=sources, unroll=8, turn=37),
+        out_shape=jax.ShapeDtypeStruct((sources * 64, 128), BF16),
+        in_specs=[pl.BlockSpec(memory_space=pltpu.SMEM), pl.BlockSpec(memory_space=VM), pl.BlockSpec(memory_space=VM)],
+        out_specs=pl.BlockSpec(memory_space=pl.ANY),
+        scratch_shapes=[
+            VM((tile_rows * tile_cols, 8, 128), F32), VM((2, 128, 1024), F32), VM((sources * 64, 128), BF16),
+            pltpu.SemaphoreType.DMA, pltpu.SemaphoreType.DMA, pltpu.SemaphoreType.DMA],
+        compiler_params=pltpu.CompilerParams(vmem_limit_bytes=48 << 20, has_side_effects=True),
+        name="serve",
+    )(idx, req, q)
+
+
+def place_kernel(idx_ref, half_ref, ret_ref, out_ref, wide_ref, x0_ref, x1_ref):
+    rows = ret_ref.shape[0]
+
+    def widen(k, _):
+        at = pl.multiple_of(k * 256, 256)
+        wide_ref[pl.ds(at, 256), :] = ret_ref[pl.ds(at, 256), :].astype(F32)
+        return 0
+
+    lax.fori_loop(0, rows // 256, widen, 0)
+
+    def fetch(k, x_ref):
+        for t in range(128):
+            x_ref[t:t + 1, :] = wide_ref[pl.ds(idx_ref[k, t], 1), :]
+
+    def work(k, x_ref):
+        y = jnp.transpose(x_ref[...])
+        second = half_ref[pl.ds(k, 1), :] > 0
+        out_ref[:, pl.ds(pl.multiple_of(k * 128, 128), 128)] = jnp.where(second, y[64:], y[:64]).astype(BF16)
+
+    blocks = half_ref.shape[0]
+    fetch(0, x0_ref)
+
+    def step(j, _):
+        k = j * 2
+        fetch(k + 1, x1_ref)
+        work(k, x0_ref)
+        fetch(jnp.minimum(k + 2, blocks - 1), x0_ref)
+        work(k + 1, x1_ref)
+        return 0
+
+    lax.fori_loop(0, blocks // 2, step, 0)
+
+
+def place(idx, half, ret):
+    n = half.shape[0] * 128
+    return pl.pallas_call(
+        place_kernel,
+        out_shape=jax.ShapeDtypeStruct((64, n), BF16),
         in_specs=[pl.BlockSpec(memory_space=pltpu.SMEM), pl.BlockSpec(memory_space=VM), pl.BlockSpec(memory_space=VM)],
         out_specs=pl.BlockSpec(memory_space=VM),
-        scratch_shapes=[VM((51 * tile_cols * 8, 128), F32), VM((1024, 128), F32), VM((1024, 128), F32)],
-        compiler_params=pltpu.CompilerParams(vmem_limit_bytes=48 << 20),
-        name="gather",
-    )(idx, req, q)
+        scratch_shapes=[VM(ret.shape, F32), VM((128, 128), F32), VM((128, 128), F32)],
+        compiler_params=pltpu.CompilerParams(vmem_limit_bytes=32 << 20),
+        name="place",
+    )(idx, half, ret)
 
 
 def shift(x, d_lat, d_lon):
@@ -297,13 +318,12 @@
     req, row, half = route(owner, offsets, fractions)
     ext = extended(grid)
     req = lax.all_to_all(req, ("lat", "lon"), split_axis=0, concat_axis=0, tiled=True)
-    idx = (req[:, :128].astype(I32) + 3 * tile_cols) * 8
+    idx = req[:, :128].astype(I32)
     read = w_read.T
     q = grid_block(
         ext, dw_kernel.reshape(49, -1), norm_gain, w_up[0], w_down[0], jnp.concatenate([read, read], axis=0),
         tile_rows * lax.axis_size("lat"), tile_rows)
-    out = gather2(idx, req, q, tile_cols)
-    ret = lax.all_to_all(out, ("lat", "lon"), split_axis=0, concat_axis=0, tiled=True)
+    ret = serve(idx, req, q, tile_rows, tile_cols, lax.axis_size("lon"))
     return place(row, half, ret).T
 
 

time: 202 us -> 182 us (0.901)
  blocking collectives: 37.7 us -> 0 us
  Pallas kernels: 99.9 us -> 118 us
    all_to_all x1 -> x0, blocking collectives: 37.7 us -> none  [shards(): lax.all_to_all(out, ('lat', 'lon'), split_axis=0, concat_axis=0, tiled=True)]
    pallas_call x1, Pallas kernels: 48 us -> 65.7 us  [serve(): pl.pallas_call(functools.partial(serve_kernel, tile_rows=tile_rows, tile_...]
  transfers between devices with their start and end apart: 9 -> 9, of which waited for: 1 -> 1; matrix products, arithmetic and copies ran while one was open for 5% -> 6% of each run, Pallas kernels for 0% -> 0%
where the time goes in v2:
time: 182 us; the launch traced here: 181 us
  Pallas kernels  118 us (65%)
  starting transfers between devices  38.7 us (21%)
  local copies, waits for them, and re-layouts  13.4 us (7%)
  other arithmetic  8.14 us (4%)
  waiting for transfers between devices  2.53 us (1%)
    pallas_call x1, Pallas kernels, serve(): pl.pallas_call(functools.partial(serve_kernel, tile_rows=tile_rows, tile_...  65.7 us
    pallas_call x1, Pallas kernels, grid_block(): pl.pallas_call(functools.partial(grid_kernel, total_rows=total_rows, tile...  33.2 us
    ppermute x8, starting transfers between devices, shift(): return lax.ppermute(x, ('lat', 'lon'), pairs)  27.2 us
    all_to_all x1, starting transfers between devices, shards(): lax.all_to_all(req, ('lat', 'lon'), split_axis=0, concat_axis=0, tiled=True)  11.5 us
    pallas_call x1, Pallas kernels, place(): pl.pallas_call(place_kernel, out_shape=jax.ShapeDtypeStruct((64, n), BF16...  9.97 us
    pallas_call x1, Pallas kernels, route(): pl.pallas_call(route_kernel, out_shape=[jax.ShapeDtypeStruct((128, 384),...  8.74 us
    concatenate x1, other arithmetic, extended(): full = jnp.concatenate([jnp.concatenate(p, axis=1) for p in parts], axis=0)  7.3 us
  transfers between devices with their start and end apart: 9, of which 1 were waited for; matrix products, arithmetic and copies ran while one was open for 6% of the time, Pallas kernels for 0%

profile of v2, /device:TPU:1, one launch (start us, length us, event | category | flops | bytes accessed | tf_op | source)
XLA Modules:
  0.0 180.6 jit_solution(15462593047841733590)
XLA Ops:
  2.4 8.7 %route.1 = (f32[128,384]{1,0:T(8,128)S(1)}, s32[64,128]{1,0:T(8,128)S(1)}, s32[64,128]{1,0:T(8,128)S(1)}) custom-call(s32[64,128]{1,0:T(8,128)S(1)} %bitcast.15, s32[64,128]{1,0:T(8,128)S(1)} %bitcast.16, f32[2,8192]{1,0:T(2,128)S(1)} %copy-done.2), custom_call_target="tpu_custom_call" | custom-call | tf_op jit(solution)/shard_map/route/pallas_call | solution.py:55
  11.1 0.9 copy.10
  12.0 11.5 %all-to-all-start = ((f32[128,1,384]{2,1,0:T(1,128)}), f32[128,1,384]{2,1,0:T(1,128)S(1)}, u32[]{:S(2)}, u32[]{:S(2)}) async-start(f32[128,1,384]{2,1,0:T(1,128)} %copy.10), calls=%async_computation | async-start | bytes 393216 | tf_op jit(solution)/shard_map/all_to_all | solution.py:320
  23.5 1.4 slice.32
  24.9 4.6 %collective-permute-start = (bf16[4,4,256]{2,1,0:T(4,128)(2,1)}, bf16[4,4,256]{2,1,0:T(4,128)(2,1)}, u32[]{:S(2)}, u32[]{:S(2)}) collective-permute-start(bf16[4,4,256]{2,1,0:T(4,128)(2,1)} %slice.32), channel_id=1, source_target_pairs={{0,17},{1,18},{2,19},{3,20},{4,21},{5,22},{6,23},{7,24},{8,25},{9,... | collective-permute-start | bytes 24584 | tf_op jit(solution)/shard_map/ppermute | solution.py:301
  29.4 1.4 slice.37
  30.8 2.7 %collective-permute-start.5 = (bf16[5,4,256]{2,1,0:T(4,128)(2,1)}, bf16[5,4,256]{2,1,0:T(4,128)(2,1)}, u32[]{:S(2)}, u32[]{:S(2)}) collective-permute-start(bf16[5,4,256]{2,1,0:T(4,128)(2,1)} %slice.37), channel_id=1, source_target_pairs={{16,1},{17,2},{18,3},{19,4},{20,5},{21,6},{22,7},{23,8},{24,9},{25... | collective-permute-start | bytes 30728 | tf_op jit(solution)/shard_map/ppermute | solution.py:301
  33.5 1.3 slice.34
  34.8 7.1 %collective-permute-start.2 = (bf16[4,5,256]{2,1,0:T(8,128)(2,1)}, bf16[4,5,256]{2,1,0:T(8,128)(2,1)}, u32[]{:S(2)}, u32[]{:S(2)}) collective-permute-start(bf16[4,5,256]{2,1,0:T(8,128)(2,1)} %slice.34), channel_id=1, source_target_pairs={{0,31},{1,16},{2,17},{3,18},{4,19},{5,20},{6,21},{7,22},{8,23},{9,... | collective-permute-start | bytes 30728 | tf_op jit(solution)/shard_map/ppermute | solution.py:301
  41.9 1.3 slice.39
  43.2 1.9 %collective-permute-start.7 = (bf16[5,5,256]{2,1,0:T(8,128)(2,1)}, bf16[5,5,256]{2,1,0:T(8,128)(2,1)S(1)}, u32[]{:S(2)}, u32[]{:S(2)}) collective-permute-start(bf16[5,5,256]{2,1,0:T(8,128)(2,1)} %slice.39), channel_id=1, source_target_pairs={{16,15},{17,0},{18,1},{19,2},{20,3},{21,4},{22,5},{23,6},{24,7},{2... | collective-permute-start | bytes 38408 | tf_op jit(solution)/shard_map/ppermute | solution.py:301
  45.2 1.0 slice.38
  46.1 1.9 %collective-permute-start.6 = (bf16[5,90,256]{2,1,0:T(8,128)(2,1)S(1)}, bf16[5,90,256]{2,1,0:T(8,128)(2,1)S(1)}, u32[]{:S(2)}, u32[]{:S(2)}) collective-permute-start(bf16[5,90,256]{2,1,0:T(8,128)(2,1)S(1)} %slice.38), channel_id=1, source_target_pairs={{16,0},{17,1},{18,2},{19,3},{20,4},{21,5},{22,6},{23,7},{24,8},{25... | collective-permute-start | bytes 691208 | tf_op jit(solution)/shard_map/ppermute | solution.py:301
  48.1 0.8 pad_maximum_fusion.read_ref
  48.9 1.1 slice.35
  50.0 0.9 slice.36
  50.9 0.9 slice.33
  53.5 4.1 %collective-permute-start.4 = (bf16[45,5,256]{2,1,0:T(8,128)(2,1)S(1)}, bf16[45,5,256]{2,1,0:T(8,128)(2,1)S(1)}, u32[]{:S(2)}, u32[]{:S(2)}) collective-permute-start(bf16[45,5,256]{2,1,0:T(8,128)(2,1)S(1)} %slice.36), channel_id=1, source_target_pairs={{0,15},{1,0},{2,1},{3,2},{4,3},{5,4},{6,5},{7,6},{8,7},{9,8},{10,9... | collective-permute-start | bytes 345608 | tf_op jit(solution)/shard_map/ppermute | solution.py:301
  57.5 4.2 %collective-permute-start.1 = (bf16[4,90,256]{2,1,0:T(8,128)(2,1)S(1)}, bf16[4,90,256]{2,1,0:T(8,128)(2,1)S(1)}, u32[]{:S(2)}, u32[]{:S(2)}) collective-permute-start(bf16[4,90,256]{2,1,0:T(8,128)(2,1)S(1)} %slice.33), channel_id=1, source_target_pairs={{0,16},{1,17},{2,18},{3,19},{4,20},{5,21},{6,22},{7,23},{8,24},{9,... | collective-permute-start | bytes 552968 | tf_op jit(solution)/shard_map/ppermute | solution.py:301
  61.8 2.5 %collective-permute-done.1 = bf16[4,90,256]{2,1,0:T(8,128)(2,1)S(1)} collective-permute-done((bf16[4,90,256]{2,1,0:T(8,128)(2,1)S(1)}, bf16[4,90,256]{2,1,0:T(8,128)(2,1)S(1)}, u32[]{:S(2)}, u32[]{:S(2)}) %collective-permute-start.1) | collective-permute-done | bytes 184352 | tf_op jit(solution)/shard_map/ppermute | solution.py:301
  64.3 7.3 %fusion.12.ext_ref = bf16[54,104,256]{2,1,0:T(8,128)(2,1)S(1)} fusion(bf16[5,5,256]{2,1,0:T(8,128)(2,1)S(1)} %collective-permute-done.7, bf16[5,90,256]{2,1,0:T(8,128)(2,1)S(1)} %collective-permute-done.6, bf16[5,4,256]{2,1,0:T(4,128)(2,1)} %collective-permute-done.5, bf16[45,5,256]{2,1,0:T(8,128)(2,1)S(1)} %collective-permute-done.4, ...), kind=kLoop, calls=%fused_computation.13 | loop fusion | flops 40255488 | bytes 5612544 | tf_op jit(solution)/shard_map/concatenate | solution.py:312
  71.7 33.2 %grid_block.1.q_ref = f32[4608,128]{1,0:T(8,128)S(1)} custom-call(bf16[54,104,256]{2,1,0:T(8,128)(2,1)S(1)} %fusion.12.ext_ref, bf16[49,256]{1,0:T(8,128)(2,1)S(1)} %reshape.13.tap_ref, f32[1,256]{1,0:T(1,128)S(1)} %copy-done.5, bf16[256,512]{1,0:T(8,128)(2,1)S(1)} %bitcast.12, bf16[512,256]{1,0:T(8,128)(2,1)S(1)} %bitcast.13, ...), custom_call_target="tpu_custom_call" | custom-call | tf_op jit(solution)/shard_map/grid_block/pallas_call | solution.py:125
  104.9 65.7 %serve.1.ret_ref = bf16[8192,128]{1,0:T(8,128)(2,1)S(1)} custom-call(s32[128,128]{1,0:T(8,128)S(1)} %slice_convert_fusion.idx_ref, f32[128,384]{1,0:T(8,128)S(1)} %bitcast.11, f32[4608,128]{1,0:T(8,128)S(1)} %grid_block.1.q_ref), custom_call_target="tpu_custom_call" | custom-call | tf_op jit(solution)/shard_map/serve/pallas_call | solution.py:235
  170.6 10.0 %place.1 = bf16[64,8192]{1,0:T(8,128)(2,1)} custom-call(s32[64,128]{1,0:T(8,128)S(1)} %get-tuple-element.8.idx_ref, s32[64,128]{1,0:T(8,128)S(1)} %get-tuple-element.9.half_ref, bf16[8192,128]{1,0:T(8,128)(2,1)S(1)} %serve.1.ret_ref), custom_call_target="tpu_custom_call" | custom-call | tf_op jit(solution)/shard_map/place/pallas_call | solution.py:283
  (26 shorter events, 4.0 us)
Async XLA Ops:
  0.0 0.8 copy-start.2
  0.8 0.8 copy-start.3
  1.6 0.8 copy-start.4
  2.4 62.0 %copy-start.6 = (bf16[45,90,256]{2,1,0:T(8,128)(2,1)S(1)}, bf16[45,90,256]{2,1,0:T(8,128)(2,1)}, u32[]{:S(2)}) copy-start(bf16[45,90,256]{2,1,0:T(8,128)(2,1)} %param.9) | copy-start | bytes 6220804
  12.0 40.6 %all-to-all-start = ((f32[128,1,384]{2,1,0:T(1,128)}), f32[128,1,384]{2,1,0:T(1,128)S(1)}, u32[]{:S(2)}, u32[]{:S(2)}) async-start(f32[128,1,384]{2,1,0:T(1,128)} %copy.10), calls=%async_computation | async-start | bytes 393216 | tf_op jit(solution)/shard_map/all_to_all | solution.py:320
  24.9 27.8 %collective-permute-start = (bf16[4,4,256]{2,1,0:T(4,128)(2,1)}, bf16[4,4,256]{2,1,0:T(4,128)(2,1)}, u32[]{:S(2)}, u32[]{:S(2)}) collective-permute-start(bf16[4,4,256]{2,1,0:T(4,128)(2,1)} %slice.32), channel_id=1, source_target_pairs={{0,17},{1,18},{2,19},{3,20},{4,21},{5,22},{6,23},{7,24},{8,25},{9,... | collective-permute-start | bytes 24584 | tf_op jit(solution)/shard_map/ppermute | solution.py:301
  30.8 22.6 %collective-permute-start.5 = (bf16[5,4,256]{2,1,0:T(4,128)(2,1)}, bf16[5,4,256]{2,1,0:T(4,128)(2,1)}, u32[]{:S(2)}, u32[]{:S(2)}) collective-permute-start(bf16[5,4,256]{2,1,0:T(4,128)(2,1)} %slice.37), channel_id=1, source_target_pairs={{16,1},{17,2},{18,3},{19,4},{20,5},{21,6},{22,7},{23,8},{24,9},{25... | collective-permute-start | bytes 30728 | tf_op jit(solution)/shard_map/ppermute | solution.py:301
  34.8 22.7 %collective-permute-start.2 = (bf16[4,5,256]{2,1,0:T(8,128)(2,1)}, bf16[4,5,256]{2,1,0:T(8,128)(2,1)}, u32[]{:S(2)}, u32[]{:S(2)}) collective-permute-start(bf16[4,5,256]{2,1,0:T(8,128)(2,1)} %slice.34), channel_id=1, source_target_pairs={{0,31},{1,16},{2,17},{3,18},{4,19},{5,20},{6,21},{7,22},{8,23},{9,... | collective-permute-start | bytes 30728 | tf_op jit(solution)/shard_map/ppermute | solution.py:301
  43.2 18.5 %collective-permute-start.7 = (bf16[5,5,256]{2,1,0:T(8,128)(2,1)}, bf16[5,5,256]{2,1,0:T(8,128)(2,1)S(1)}, u32[]{:S(2)}, u32[]{:S(2)}) collective-permute-start(bf16[5,5,256]{2,1,0:T(8,128)(2,1)} %slice.39), channel_id=1, source_target_pairs={{16,15},{17,0},{18,1},{19,2},{20,3},{21,4},{22,5},{23,6},{24,7},{2... | collective-permute-start | bytes 38408 | tf_op jit(solution)/shard_map/ppermute | solution.py:301
  46.1 18.2 %collective-permute-start.6 = (bf16[5,90,256]{2,1,0:T(8,128)(2,1)S(1)}, bf16[5,90,256]{2,1,0:T(8,128)(2,1)S(1)}, u32[]{:S(2)}, u32[]{:S(2)}) collective-permute-start(bf16[5,90,256]{2,1,0:T(8,128)(2,1)S(1)} %slice.38), channel_id=1, source_target_pairs={{16,0},{17,1},{18,2},{19,3},{20,4},{21,5},{22,6},{23,7},{24,8},{25... | collective-permute-start | bytes 691208 | tf_op jit(solution)/shard_map/ppermute | solution.py:301
  52.7 9.1 %collective-permute-start.3 = (bf16[45,4,256]{2,1,0:T(4,128)(2,1)S(1)}, bf16[45,4,256]{2,1,0:T(4,128)(2,1)S(1)}, u32[]{:S(2)}, u32[]{:S(2)}) collective-permute-start(bf16[45,4,256]{2,1,0:T(4,128)(2,1)S(1)} %slice.35), channel_id=1, source_target_pairs={{0,1},{1,2},{2,3},{3,4},{4,5},{5,6},{6,7},{7,8},{8,9},{9,10},{10,1... | collective-permute-start | bytes 276488 | tf_op jit(solution)/shard_map/ppermute | solution.py:301
  53.5 8.3 %collective-permute-start.4 = (bf16[45,5,256]{2,1,0:T(8,128)(2,1)S(1)}, bf16[45,5,256]{2,1,0:T(8,128)(2,1)S(1)}, u32[]{:S(2)}, u32[]{:S(2)}) collective-permute-start(bf16[45,5,256]{2,1,0:T(8,128)(2,1)S(1)} %slice.36), channel_id=1, source_target_pairs={{0,15},{1,0},{2,1},{3,2},{4,3},{5,4},{6,5},{7,6},{8,7},{9,8},{10,9... | collective-permute-start | bytes 345608 | tf_op jit(solution)/shard_map/ppermute | solution.py:301
  57.5 6.8 %collective-permute-start.1 = (bf16[4,90,256]{2,1,0:T(8,128)(2,1)S(1)}, bf16[4,90,256]{2,1,0:T(8,128)(2,1)S(1)}, u32[]{:S(2)}, u32[]{:S(2)}) collective-permute-start(bf16[4,90,256]{2,1,0:T(8,128)(2,1)S(1)} %slice.33), channel_id=1, source_target_pairs={{0,16},{1,17},{2,18},{3,19},{4,20},{5,21},{6,22},{7,23},{8,24},{9,... | collective-permute-start | bytes 552968 | tf_op jit(solution)/shard_map/ppermute | solution.py:301
  61.7 9.9 %copy-start = (bf16[1,256,512]{2,1,0:T(8,128)(2,1)S(1)}, bf16[1,256,512]{2,1,0:T(8,128)(2,1)}, u32[]{:S(2)}) copy-start(bf16[1,256,512]{2,1,0:T(8,128)(2,1)} %param.12) | copy-start | bytes 786436
  61.8 9.9 %copy-start.1 = (bf16[1,512,256]{2,1,0:T(8,128)(2,1)S(1)}, bf16[1,512,256]{2,1,0:T(8,128)(2,1)}, u32[]{:S(2)}) copy-start(bf16[1,512,256]{2,1,0:T(8,128)(2,1)} %param.13) | copy-start | bytes 786436
  61.8 9.9 %copy-start.5 = (f32[1,256]{1,0:T(1,128)S(1)}, f32[1,256]{1,0:T(1,128)}, u32[]{:S(2)}) copy-start(f32[1,256]{1,0:T(1,128)} %gain_ref.1) | copy-start | bytes 3076

commit v3 on v2

v3 whole, which is shorter than its diff:
```python
import functools
import jax, jax.numpy as jnp
from jax import lax
from jax.experimental import pallas as pl
from jax.experimental.pallas import tpu as pltpu
from jax.sharding import PartitionSpec as P
F32, BF16, I32 = jnp.float32, jnp.bfloat16, jnp.int32
VM = pltpu.VMEM

COLS, EXT = 96, 112


def route_body(owner_ref, off_ref, fr_ref, req_ref, row_ref, half_ref, hot_ref, val_ref):
    blocks = owner_ref.shape[0]
    sub = lax.broadcasted_iota(I32, (128, 128), 0)
    lane = lax.broadcasted_iota(I32, (128, 128), 1)
    upper = jnp.where(sub < lane, 1.0, 0.0).astype(BF16)
    prefix = jnp.concatenate([upper, jnp.ones((128, 128), BF16)], axis=1)
    group = 8

    def step(k, base):
        for u in range(group):
            b = k * group + u
            mine = owner_ref[pl.ds(b, 1), :]
            hot = jnp.where(mine == sub, 1.0, 0.0)
            hot16 = hot.astype(BF16)
            hot_ref[:, u * 128:(u + 1) * 128] = hot16
            sums = jnp.dot(hot16, prefix, preferred_element_type=F32)
            ranks = jnp.sum((sums[:, :128] + base) * hot, axis=0, keepdims=True)
            base = base + sums[:, 128:]
            rank = ranks.astype(I32)
            row_ref[pl.ds(b, 1), :] = jnp.clip(mine, 0, 127) * 64 + (rank & 63)
            half_ref[pl.ds(b, 1), :] = rank >> 6
            there = rank == sub
            off = off_ref[pl.ds(b, 1), :]
            fy = fr_ref[0:1, pl.ds(pl.multiple_of(b * 128, 128), 128)]
            fx = fr_ref[1:2, pl.ds(pl.multiple_of(b * 128, 128), 128)]
            fy_hi = fy.astype(BF16).astype(F32)
            fx_hi = fx.astype(BF16).astype(F32)
            parts = [(off >> 6).astype(F32), (off & 63).astype(F32), fy_hi, fy - fy_hi, fx_hi, fx - fx_hi]
            for p, part in enumerate(parts):
                val_ref[p * 128:(p + 1) * 128, u * 128:(u + 1) * 128] = jnp.where(there, part, 0.0).astype(BF16)
        acc = lax.dot_general(hot_ref[...], val_ref[...], (((1,), (1,)), ((), ())), preferred_element_type=F32)
        new = [acc[:, 0:128] * 64.0 + acc[:, 128:256], acc[:, 256:384] + acc[:, 384:512], acc[:, 512:640] + acc[:, 640:768]]
        for q in range(3):
            at = pl.ds(q, 128, stride=8)
            req_ref[at, :] = jnp.where(k == 0, new[q], req_ref[at, :] + new[q])
        return base

    lax.fori_loop(0, blocks // group, step, jnp.zeros((128, 128), F32))


def grid_body(x_ref, tap8_ref, mix_ref, gain_ref, up_ref, down_ref, read_ref, q_ref, first, total_rows):
    for h in range(2):
        def conv(c, _):
            acc = [None] * 6
            for b in range(7):
                x = [x_ref[h, pl.ds(pl.multiple_of((rr * EXT + c + 4 + b) * 8, 8), 8), :] for rr in range(12)]
                for a in range(7):
                    t = a * 7 + b
                    k = tap8_ref[h, t * 8:(t + 1) * 8, :]
                    for r in range(6):
                        p = x[r + a] * k
                        acc[r] = p if acc[r] is None else acc[r] + p
            for r in range(6):
                mix_ref[pl.ds(pl.multiple_of((r * COLS + c) * 8, 8), 8), h * 128:(h + 1) * 128] = acc[r]
            return 0

        lax.fori_loop(0, COLS, conv, 0)

    n = COLS * 8
    low = lax.broadcasted_iota(I32, (n, 128), 1) < 64
    strip = lax.broadcasted_iota(I32, (n, 128), 0) & 7

    def mlp(r, _):
        at = pl.multiple_of(r * n, n)
        m = mix_ref[pl.ds(at, n), :]
        m = m - jnp.mean(m, axis=1, keepdims=True)
        var = jnp.mean(m * m, axis=1, keepdims=True)
        normed = (m * lax.rsqrt(var + 1e-6) * gain_ref[...]).astype(BF16)
        hidden = jax.nn.gelu(jnp.dot(normed, up_ref[...], preferred_element_type=F32)).astype(BF16)
        delta = jnp.dot(hidden, down_ref[...], preferred_element_type=F32)
        mid = pl.multiple_of(((r + 3) * EXT + 7) * 8, 8)
        centre = jnp.concatenate([x_ref[0, pl.ds(mid, n), :], x_ref[1, pl.ds(mid, n), :]], axis=1)
        field = (centre + delta).astype(BF16)
        p = lax.dot_general(field, read_ref[...], (((1,), (1,)), ((), ())), preferred_element_type=F32)
        p = p.astype(BF16).astype(F32)
        row = first + strip * 6 + r
        p = jnp.where((row >= 0) & (row < total_rows), p, 0.0)
        q_ref[pl.ds(at, n), :] = jnp.where(low, p, jnp.concatenate([p[8:], p[:8]], axis=0))
        return 0

    lax.fori_loop(0, 6, mlp, 0)


def flat_weights(fr_ref, w_ref):
    fy, fx = fr_ref[0], fr_ref[1]
    a = [jnp.exp(-fy - 0.5), jnp.ones_like(fy), jnp.exp(fy - 0.5), jnp.exp(fy + fy - 2.0)]
    b = [jnp.exp(-fx - 0.5), jnp.ones_like(fx), jnp.exp(fx - 0.5), jnp.exp(fx + fx - 2.0)]
    scale = 1.0 / ((a[0] + a[1] + a[2] + a[3]) * (b[0] + b[1] + b[2] + b[3]))
    a = [x * scale for x in a]
    row = lax.broadcasted_iota(I32, (128, 1024), 0)
    col = lax.broadcasted_iota(I32, (128, 1024), 1)
    for s in range(8):
        one = jnp.where(col == row * 8 + s, 1.0, 0.0).astype(BF16)
        for half in range(2):
            plane = (a[s // 2] * b[2 * (s % 2) + half]).astype(BF16)
            part = jnp.dot(plane, one, preferred_element_type=F32)
            w_ref[half] = part if s == 0 else w_ref[half] + part


def build_table(q_ref, table_ref, tile_rows, tile_cols):
    sub = lax.broadcasted_iota(I32, (8, 128), 0)
    masks = {n: (sub & n) == 0 for n in (1, 2, 4)}

    def build(c, _):
        q = [[None] * 2 for _ in range(9)]
        for jj in range(2):
            for r in range(6):
                q[r][jj] = q_ref[pl.ds(pl.multiple_of((r * COLS + c + 2 * jj) * 8, 8), 8), :]
            for r in range(3):
                q[r + 6][jj] = pltpu.roll(q[r][jj], 7, 0)
        for r in range(6):
            v = [q[r + i][jj] for i in range(4) for jj in range(2)]
            for n in (4, 2, 1):
                new = list(v)
                for k in range(8):
                    if not k & n:
                        new[k] = jnp.where(masks[n], v[k], pltpu.roll(v[k + n], n, 0))
                        new[k + n] = jnp.where(masks[n], pltpu.roll(v[k], 8 - n, 0), v[k + n])
                v = new
            for k in range(8):
                if 6 * k + r < tile_rows:
                    table_ref[(6 * k + r) * tile_cols + c] = v[k]
        return 0

    lax.fori_loop(0, tile_cols, build, 0)


def read_source(idx_ref, d, table_ref, w_ref, out_ref, low):
    own = (lax.broadcasted_iota(I32, (32, 256), 1) >> 3) == lax.broadcasted_iota(I32, (32, 256), 0)
    sums = []
    for g in range(4):
        patches = []
        for s in range(32):
            patches.append(table_ref[idx_ref[d, g * 32 + s]])
        weights = [jnp.where(own, w_ref[h, pl.ds(d, 1), g * 256:(g + 1) * 256], 0.0) for h in range(2)]
        sums.append(jnp.dot(
            jnp.concatenate(weights, axis=0).astype(BF16), jnp.concatenate(patches, axis=0).astype(BF16),
            preferred_element_type=F32))
    for g in range(2):
        first, second = sums[g], sums[g + 2]
        keep = jnp.where(low, first[:32], second[32:])
        move = jnp.where(low, second[:32], first[32:])
        at = pl.multiple_of(d * 64 + g * 32, 32)
        out_ref[pl.ds(at, 32), :] = (keep + pltpu.roll(move, 64, 1)).astype(BF16)


def place_body(idx_ref, half_ref, ret_ref, out_ref, wide_ref, x0_ref, x1_ref):
    rows = ret_ref.shape[0]

    def widen(k, _):
        at = pl.multiple_of(k * 256, 256)
        wide_ref[pl.ds(at, 256), :] = ret_ref[pl.ds(at, 256), :].astype(F32)
        return 0

    lax.fori_loop(0, rows // 256, widen, 0)

    def fetch(k, x_ref):
        for t in range(128):
            x_ref[t:t + 1, :] = wide_ref[pl.ds(idx_ref[k, t], 1), :]

    def work(k, x_ref):
        y = jnp.transpose(x_ref[...])
        second = half_ref[pl.ds(k, 1), :] > 0
        out_ref[:, pl.ds(pl.multiple_of(k * 128, 128), 128)] = jnp.where(second, y[64:], y[:64]).astype(BF16)

    blocks = half_ref.shape[0]
    fetch(0, x0_ref)

    def step(j, _):
        k = j * 2
        fetch(k + 1, x1_ref)
        work(k, x0_ref)
        fetch(jnp.minimum(k + 2, blocks - 1), x0_ref)
        work(k + 1, x1_ref)
        return 0

    lax.fori_loop(0, blocks // 2, step, 0)


def window_kernel(
    owner_ref, off_ref, fr_ref, grid_ref, tap_ref, gain_ref, up_ref, down_ref, read_ref, result_ref,
    hot_ref, val_ref, req_ref, got_ref, east_ref, west_ref, left_ref, right_ref, top_ref, bottom_ref, corner_ref,
    x_ref, tap8_ref, mix_ref, q_ref, row_ref, half_ref, idx_ref, where_ref, table_ref, w_ref, out_ref, ret_ref, wide_ref,
    x0_ref, x1_ref, idx_smem, row_smem,
    send_sem, recv_sem, req_send, req_recv, own_sem, val_send, val_recv, idx_sem, row_sem, *, n_lat, n_lon, turn, unroll):
    lat, lon = lax.axis_index("lat"), lax.axis_index("lon")
    me = lat * n_lon + lon
    devices = n_lat * n_lon
    tile_rows, tile_cols = grid_ref.shape[:2]
    first = lat * tile_rows - 1

    def partner(k):
        d = lax.rem(me + k * turn, devices)
        return d, (lax.div(d, n_lon), lax.rem(d, n_lon))

    barrier = pltpu.get_barrier_semaphore()

    def hello(k, _):
        pl.semaphore_signal(barrier, inc=1, device_id=partner(k)[1], device_id_type=pl.DeviceIdType.MESH)
        return 0

    lax.fori_loop(1, devices, hello, 0)

    def pack(k, _):
        a = grid_ref[2 * k].astype(F32)
        b = grid_ref[jnp.minimum(2 * k + 1, tile_rows - 1)].astype(F32)
        at = pl.ds(pl.multiple_of(k * 16, 16), 16)
        east_ref[at, :] = jnp.concatenate([a[tile_cols - 8:], b[tile_cols - 8:]], axis=0).astype(BF16)
        west_ref[at, :] = jnp.concatenate([a[:8], b[:8]], axis=0).astype(BF16)
        return 0

    pairs = (tile_rows + 1) // 2
    lax.fori_loop(0, pairs, pack, 0)
    up = lax.rem(lat + n_lat - 1, n_lat)
    down = lax.rem(lat + 1, n_lat)
    prev = lax.rem(lon + n_lon - 1, n_lon)
    post = lax.rem(lon + 1, n_lon)
    low_rows, high_rows = pl.ds((pairs - 3) * 16, 48), pl.ds(0, 48)
    moves = [
        (grid_ref.at[pl.ds(tile_rows - 4, 4)], top_ref, (down, lon)),
        (grid_ref.at[pl.ds(0, 5)], bottom_ref, (up, lon)),
        (east_ref, left_ref, (lat, post)),
        (west_ref, right_ref, (lat, prev)),
        (east_ref.at[low_rows], corner_ref.at[0], (down, post)),
        (west_ref.at[low_rows], corner_ref.at[1], (down, prev)),
        (east_ref.at[high_rows], corner_ref.at[2], (up, post)),
        (west_ref.at[high_rows], corner_ref.at[3], (up, prev)),
    ]
    halos = [
        pltpu.make_async_remote_copy(src_ref=a, dst_ref=b, send_sem=send_sem.at[n], recv_sem=recv_sem.at[n], device_id=to,
                                     device_id_type=pl.DeviceIdType.MESH)
        for n, (a, b, to) in enumerate(moves)
    ]
    route_body(owner_ref, off_ref, fr_ref, req_ref, row_ref, half_ref, hot_ref, val_ref)
    rows_in = pltpu.make_async_copy(row_ref, row_smem, row_sem)
    rows_in.start()
    pl.semaphore_wait(barrier, devices - 1)
    for h in halos:
        h.start()

    def eight(d):
        return pl.ds(pl.multiple_of(d * 8, 8), 8)

    own = pltpu.make_async_copy(req_ref.at[eight(me)], got_ref.at[eight(me)], own_sem)
    own.start()

    def ask(k, _):
        d, to = partner(k)
        pltpu.make_async_remote_copy(
            src_ref=req_ref.at[eight(d)], dst_ref=got_ref.at[eight(me)], send_sem=req_send, recv_sem=req_recv,
            device_id=to, device_id_type=pl.DeviceIdType.MESH).start()
        return 0

    lax.fori_loop(1, devices, ask, 0)

    def put(h, r, c, s, v):
        x_ref[h, pl.ds((r * EXT + c) * 8 + s, v.shape[0], stride=8), :] = v

    def put_row(r, s, v):
        for h in range(2):
            for c in range(0, tile_cols, 8):
                put(h, r, c + 8, s, v[c:min(c + 8, tile_cols), h * 128:(h + 1) * 128])

    def put_side(r, s, v, c):
        for h in range(2):
            put(h, r, c, s, v[:, h * 128:(h + 1) * 128])

    for r in range(12):
        if r >= 4:
            put_row(r, 0, grid_ref[r - 4].astype(F32))
        if r <= tile_rows - 39:
            put_row(r, 7, grid_ref[38 + r].astype(F32))

    def relay(r, _):
        for s in range(1, 7):
            put_row(r, s, grid_ref[6 * s + r - 4].astype(F32))
        return 0

    lax.fori_loop(0, 12, relay, 0)
    for h in range(2):
        for t in range(49):
            tap8_ref[h, t * 8:(t + 1) * 8, :] = jnp.broadcast_to(tap_ref[t:t + 1, h * 128:(h + 1) * 128].astype(F32), (8, 128))

    for h in halos:
        h.wait()
    above = jnp.where(lat > 0, 1.0, 0.0)
    below = jnp.where(lat < n_lat - 1, 1.0, 0.0)

    def block(ref, k):
        return ref[pl.ds(pl.multiple_of(k * 16, 16), 16), :].astype(F32)

    def sides(r2, s):
        k = 3 * s + r2 - 2
        a, b = block(left_ref, k), block(right_ref, k)
        for u in range(2):
            put_side(2 * r2 + u, s, a[8 * u:8 * u + 8], 0)
            put_side(2 * r2 + u, s, b[8 * u:8 * u + 8], tile_cols + 8)

    def middle(r2, _):
        for s in range(1, 7):
            sides(r2, s)
        return 0

    lax.fori_loop(0, 6, middle, 0)
    for r2 in range(2, 6):
        sides(r2, 0)
    for r2 in range(0, 4):
        sides(r2, 7)
    for r in range(4):
        put_row(r, 0, top_ref[r].astype(F32) * above)
        for n, c in ((0, 0), (1, tile_cols + 8)):
            v = corner_ref[n, (r + 1) // 2 * 16:(r + 1) // 2 * 16 + 16, :].astype(F32) * above
            put_side(r, 0, v[(r + 1) % 2 * 8:(r + 1) % 2 * 8 + 8], c)
    for r in range(7, 12):
        put_row(r, 7, bottom_ref[r - 7].astype(F32) * below)
        for n, c in ((2, 0), (3, tile_cols + 8)):
            v = corner_ref[n, (r - 7) // 2 * 16:(r - 7) // 2 * 16 + 16, :].astype(F32) * below
            put_side(r, 7, v[(r - 7) % 2 * 8:(r - 7) % 2 * 8 + 8], c)

    grid_body(x_ref, tap8_ref, mix_ref, gain_ref, up_ref, down_ref, read_ref, q_ref, first, tile_rows * n_lat)

    own.wait()
    most = pl.ds(0, (devices - 1) * 8)
    pltpu.make_async_copy(req_ref.at[most], got_ref.at[most], req_send).wait()
    pltpu.make_async_copy(req_ref.at[most], got_ref.at[most], req_recv).wait()
    cells = got_ref[pl.ds(0, devices, stride=8), :].astype(I32)
    idx_ref[...] = jnp.clip(cells, 0, tile_rows * tile_cols - 1)
    where_ref[0] = got_ref[pl.ds(1, devices, stride=8), :]
    where_ref[1] = got_ref[pl.ds(2, devices, stride=8), :]
    idx_in = pltpu.make_async_copy(idx_ref, idx_smem, idx_sem)
    idx_in.start()
    flat_weights(where_ref, w_ref)
    build_table(q_ref, table_ref, tile_rows, tile_cols)
    idx_in.wait()

    low = lax.broadcasted_iota(I32, (32, 128), 1) < 64

    def rows(d):
        return pl.ds(pl.multiple_of(d * 64, 64), 64)

    mine = pltpu.make_async_copy(out_ref.at[rows(me)], ret_ref.at[rows(me)], own_sem)

    def send(d, to):
        pltpu.make_async_remote_copy(
            src_ref=out_ref.at[rows(d)], dst_ref=ret_ref.at[rows(me)], send_sem=val_send, recv_sem=val_recv,
            device_id=to, device_id_type=pl.DeviceIdType.MESH).start()

    def serve(j, _):
        for u in range(unroll):
            d, to = partner(j * unroll + u)
            read_source(idx_smem, d, table_ref, w_ref, out_ref, low)
            if u:
                send(d, to)
            else:
                pl.when(j > 0)(functools.partial(send, d, to))
                pl.when(j == 0)(mine.start)
        return 0

    lax.fori_loop(0, devices // unroll, serve, 0)
    mine.wait()
    rows_in.wait()
    most = pl.ds(0, (devices - 1) * 64)
    pltpu.make_async_copy(out_ref.at[most], ret_ref.at[most], val_send).wait()
    pltpu.make_async_copy(out_ref.at[most], ret_ref.at[most], val_recv).wait()
    place_body(row_smem, half_ref, ret_ref, result_ref, wide_ref, x0_ref, x1_ref)


def window(owner, offsets, fractions, grid, taps, gain, up, down, read2, n_lat, n_lon):
    n = owner.shape[0] // 128
    devices = n_lat * n_lon
    tile_rows, tile_cols = grid.shape[:2]
    pairs = (tile_rows + 1) // 2
    dma = pltpu.SemaphoreType.DMA
    return pl.pallas_call(
        functools.partial(window_kernel, n_lat=n_lat, n_lon=n_lon, turn=37, unroll=8),
        out_shape=jax.ShapeDtypeStruct((64, n * 128), BF16),
        in_specs=[pl.BlockSpec(memory_space=VM)] * 9,
        out_specs=pl.BlockSpec(memory_space=VM),
        scratch_shapes=[
            VM((128, 1024), BF16), VM((768, 1024), BF16), VM((devices * 8, 128), F32), VM((devices * 8, 128), F32),
            VM((pairs * 16, 256), BF16), VM((pairs * 16, 256), BF16), VM((pairs * 16, 256), BF16), VM((pairs * 16, 256), BF16),
            VM((4, tile_cols, 256), BF16), VM((5, tile_cols, 256), BF16), VM((4, 48, 256), BF16),
            VM((2, 12 * EXT * 8, 128), F32), VM((2, 49 * 8, 128), F32), VM((6 * COLS * 8, 256), F32),
            VM((6 * COLS * 8, 128), F32), VM((n, 128), I32), VM((n, 128), I32), VM((devices, 128), I32), VM((2, devices, 128), F32),
            VM((tile_rows * tile_cols, 8, 128), F32), VM((2, devices, 1024), F32), VM((devices * 64, 128), BF16),
            VM((devices * 64, 128), BF16), VM((devices * 64, 128), F32), VM((128, 128), F32), VM((128, 128), F32),
            pltpu.SMEM((devices, 128), I32), pltpu.SMEM((n, 128), I32),
            dma((8,)), dma((8,)), dma, dma, dma, dma, dma, dma, dma],
        compiler_params=pltpu.CompilerParams(vmem_limit_bytes=60 << 20, has_side_effects=True, collective_id=0),
        name="window",
    )(owner.reshape(n, 128), offsets.reshape(n, 128), fractions, grid, taps, gain, up, down, read2)


def shards(grid, dw_kernel, norm_gain, w_up, w_down, w_read, owner, offsets, fractions):
    n_lat, n_lon = lax.axis_size("lat"), lax.axis_size("lon")
    read = w_read.T
    return window(
        owner, offsets, fractions, grid, dw_kernel.reshape(49, -1), norm_gain, w_up[0], w_down[0],
        jnp.concatenate([read, read], axis=0), n_lat, n_lon).T


def solution(mesh):
    return jax.shard_map(
        shards,
        mesh=mesh,
        in_specs=(P("lat", "lon", None), P(), P(), P(), P(), P(), P(("lat", "lon"), None), P(("lat", "lon")), P(None, ("lat", "lon"))),
        out_specs=P(("lat", "lon"), None),
        check_vma=False,
    )
```

time: 182 us -> 125 us (0.69)
  starting transfers between devices: 38.7 us -> 0 us
  local copies, waits for them, and re-layouts: 13.4 us -> 3.63 us
  other arithmetic: 8.14 us -> 1.47 us
  waiting for transfers between devices: 2.53 us -> 0 us
  Pallas kernels: 118 us -> 120 us
    ppermute x8 -> x0, starting transfers between devices: 27.2 us -> none  [shift(): return lax.ppermute(x, ('lat', 'lon'), pairs)]
    all_to_all x1 -> x0, starting transfers between devices: 11.5 us -> none  [shards(): lax.all_to_all(req, ('lat', 'lon'), split_axis=0, concat_axis=0, tiled=True)]
    slice x8 -> x0, local copies, waits for them, and re-layouts: 9.31 us -> none  [the longest x2 1.91 us: extended(): top, bottom = (grid[rows - 4:], grid[:5])]
    concatenate x1 -> x0, other arithmetic: 7.3 us -> none  [extended(): full = jnp.concatenate([jnp.concatenate(p, axis=1) for p in parts], axis=0)]
    ppermute x8 -> x0, waiting for transfers between devices: 2.53 us -> none  [shift(): return lax.ppermute(x, ('lat', 'lon'), pairs)]
    pallas_call x4 -> x1, Pallas kernels: 118 us -> 120 us  [window(): pl.pallas_call(functools.partial(window_kernel, n_lat=n_lat, n_lon=n_lon,...]
  transfers between devices with their start and end apart: 9 -> 0, of which waited for: 1 -> 0; matrix products, arithmetic and copies ran while one was open for 6% -> 0% of each run, Pallas kernels for 0% -> 0%
where the time goes in v3:
time: 125 us
  Pallas kernels  120 us (96%)
  local copies, waits for them, and re-layouts  3.63 us (3%)
  other arithmetic  1.47 us (1%)
    pallas_call x1, Pallas kernels, window(): pl.pallas_call(functools.partial(window_kernel, n_lat=n_lat, n_lon=n_lon,...  120 us

profile of v3, /device:TPU:1, one launch (start us, length us, event | category | flops | bytes accessed | tf_op | source)
XLA Modules:
  0.0 124.8 jit_solution(17338862850477509701)
XLA Ops:
  0.0 1.4 %reshape.11.tap_ref = bf16[49,256]{1,0:T(8,128)(2,1)} reshape(bf16[1,7,7,256]{3,2,1,0:T(8,128)(2,1)} %param.10) | data formatting | bytes 50176 | tf_op jit(solution)/shard_map/reshape | solution.py:410
  1.4 1.5 %pad_maximum_fusion.read_ref = bf16[128,256]{1,0:T(8,128)(2,1)} fusion(bf16[64,256]{1,0:T(8,128)(2,1)} %bitcast.11), kind=kLoop, calls=%fused_computation | loop fusion | flops 131072 | bytes 98304 | tf_op jit(solution)/shard_map/concatenate | solution.py:411
  2.8 119.7 %window.1 = bf16[64,8192]{1,0:T(8,128)(2,1)} custom-call(s32[64,128]{1,0:T(8,128)} %bitcast.9, s32[64,128]{1,0:T(8,128)} %bitcast.10, f32[2,8192]{1,0:T(2,128)} %fr_ref.1, bf16[45,90,256]{2,1,0:T(8,128)(2,1)} %grid_ref.1, bf16[49,256]{1,0:T(8,128)(2,1)} %reshape.11.tap_ref, f32[1,256]{1,0:T(1,128)} %gain_ref.1, bf16[256,512]{1,0:T(8,128)(2,1)} %bitcast.7, ...), custom_call_target="tpu_custom_call" | custom-call | tf_op jit(solution)/shard_map/window/pallas_call | solution.py:386
  122.5 2.3 %copy.11 = bf16[8192,64]{0,1:T(8,128)(2,1)} copy(bf16[8192,64]{0,1:T(8,128)(2,1)} %bitcast.6) | data formatting | bytes 2097152

commit v4 on v3

--- a/solution.py
+++ b/solution.py
@@ -8,6 +8,8 @@
 VM = pltpu.VMEM
 
 COLS, EXT = 96, 112
+PAIRS = COLS // 2
+SPLIT = 3
 
 
 def route_body(owner_ref, off_ref, fr_ref, req_ref, row_ref, half_ref, hot_ref, val_ref):
@@ -50,31 +52,77 @@
     lax.fori_loop(0, blocks // group, step, jnp.zeros((128, 128), F32))
 
 
-def grid_body(x_ref, tap8_ref, mix_ref, gain_ref, up_ref, down_ref, read_ref, q_ref, first, total_rows):
+def tap_bands(tap_ref, band_ref):
+    eye = lax.broadcasted_iota(I32, (128, 128), 0) == lax.broadcasted_iota(I32, (128, 128), 1)
     for h in range(2):
-        def conv(c, _):
-            acc = [None] * 6
-            for b in range(7):
-                x = [x_ref[h, pl.ds(pl.multiple_of((rr * EXT + c + 4 + b) * 8, 8), 8), :] for rr in range(12)]
-                for a in range(7):
-                    t = a * 7 + b
-                    k = tap8_ref[h, t * 8:(t + 1) * 8, :]
-                    for r in range(6):
-                        p = x[r + a] * k
-                        acc[r] = p if acc[r] is None else acc[r] + p
-            for r in range(6):
-                mix_ref[pl.ds(pl.multiple_of((r * COLS + c) * 8, 8), 8), h * 128:(h + 1) * 128] = acc[r]
+        def fill(a, _):
+            for j in range(8):
+                for o in range(2):
+                    if 0 <= j - o < 7:
+                        taps = tap_ref[a, j - o:j - o + 1, h * 128:(h + 1) * 128].astype(F32)
+                        block = jnp.where(eye, taps, 0.0).astype(BF16)
+                    else:
+                        block = jnp.zeros((128, 128), BF16)
+                    band_ref[h, a, j * 128:(j + 1) * 128, o * 128:(o + 1) * 128] = block
             return 0
 
-        lax.fori_loop(0, COLS, conv, 0)
-
+        lax.fori_loop(0, SPLIT, fill, 0)
+
+
+def pack_pairs(x_ref, pack_ref):
+    def step(r, _):
+        for h in range(2):
+            for par in range(2):
+                for m in range(PAIRS // 2 + 2):
+                    v = [x_ref[h, pl.ds(pl.multiple_of((r * EXT + 2 * (2 * m + n + 2) + par) * 8, 8), 8), :] for n in range(3)]
+                    pack_ref[0, h, par, r, m * 16:m * 16 + 16, :] = jnp.concatenate(v[:2], axis=0).astype(BF16)
+                    pack_ref[1, h, par, r, m * 16:m * 16 + 16, :] = jnp.concatenate(v[1:], axis=0).astype(BF16)
+        return 0
+
+    lax.fori_loop(0, 12, step, 0)
+
+
+def conv_body(x_ref, tap8_ref, pack_ref, band_ref, part_ref, mix_ref, split):
+    n = PAIRS * 8
+    for h in range(2):
+        def conv(r, _):
+            for c0 in range(0, COLS, 6):
+                acc = [None] * 6
+                for a in range(split, 7):
+                    x = [x_ref[h, pl.ds(pl.multiple_of(((r + a) * EXT + c0 + 4 + c) * 8, 8), 8), :] for c in range(12)]
+                    for b in range(7):
+                        k = tap8_ref[h, (a * 7 + b) * 8:(a * 7 + b) * 8 + 8, :]
+                        for c in range(6):
+                            p = x[c + b] * k
+                            acc[c] = p if acc[c] is None else acc[c] + p
+                for c in range(6):
+                    part_ref[(c0 + c) % 2, (c0 + c) // 2 * 8:(c0 + c) // 2 * 8 + 8, :] = acc[c]
+            acc = None
+            for a in range(split):
+                parts = []
+                for q in range(4):
+                    for par in range(2):
+                        parts.append(pack_ref[q % 2, h, par, r + a, (q // 2) * 16:(q // 2) * 16 + n, :])
+                p = jnp.dot(jnp.concatenate(parts, axis=1), band_ref[h, a], preferred_element_type=F32)
+                acc = p if acc is None else acc + p
+            for o in range(2):
+                both = acc[:, o * 128:(o + 1) * 128] + part_ref[o]
+                mix_ref[r, :, o, :, h * 128:(h + 1) * 128] = both.reshape(PAIRS, 8, 128)
+            return 0
+
+        lax.fori_loop(0, 6, conv, 0)
+
+
+def grid_body(x_ref, tap8_ref, pack_ref, band_ref, part_ref, mix_ref, gain_ref, up_ref, down_ref, read_ref, q_ref, first, total_rows):
+    conv_body(x_ref, tap8_ref, pack_ref, band_ref, part_ref, mix_ref, SPLIT)
+    read = jnp.concatenate([read_ref[...], read_ref[...]], axis=0)
     n = COLS * 8
     low = lax.broadcasted_iota(I32, (n, 128), 1) < 64
     strip = lax.broadcasted_iota(I32, (n, 128), 0) & 7
 
     def mlp(r, _):
         at = pl.multiple_of(r * n, n)
-        m = mix_ref[pl.ds(at, n), :]
+        m = mix_ref[r].reshape(n, 256)
         m = m - jnp.mean(m, axis=1, keepdims=True)
         var = jnp.mean(m * m, axis=1, keepdims=True)
         normed = (m * lax.rsqrt(var + 1e-6) * gain_ref[...]).astype(BF16)
@@ -83,7 +131,7 @@
         mid = pl.multiple_of(((r + 3) * EXT + 7) * 8, 8)
         centre = jnp.concatenate([x_ref[0, pl.ds(mid, n), :], x_ref[1, pl.ds(mid, n), :]], axis=1)
         field = (centre + delta).astype(BF16)
-        p = lax.dot_general(field, read_ref[...], (((1,), (1,)), ((), ())), preferred_element_type=F32)
+        p = lax.dot_general(field, read, (((1,), (1,)), ((), ())), preferred_element_type=F32)
         p = p.astype(BF16).astype(F32)
         row = first + strip * 6 + r
         p = jnp.where((row >= 0) & (row < total_rows), p, 0.0)
@@ -156,16 +204,7 @@
         out_ref[pl.ds(at, 32), :] = (keep + pltpu.roll(move, 64, 1)).astype(BF16)
 
 
-def place_body(idx_ref, half_ref, ret_ref, out_ref, wide_ref, x0_ref, x1_ref):
-    rows = ret_ref.shape[0]
-
-    def widen(k, _):
-        at = pl.multiple_of(k * 256, 256)
-        wide_ref[pl.ds(at, 256), :] = ret_ref[pl.ds(at, 256), :].astype(F32)
-        return 0
-
-    lax.fori_loop(0, rows // 256, widen, 0)
-
+def place_body(idx_ref, half_ref, wide_ref, out_ref, x0_ref, x1_ref):
     def fetch(k, x_ref):
         for t in range(128):
             x_ref[t:t + 1, :] = wide_ref[pl.ds(idx_ref[k, t], 1), :]
@@ -192,7 +231,7 @@
 def window_kernel(
     owner_ref, off_ref, fr_ref, grid_ref, tap_ref, gain_ref, up_ref, down_ref, read_ref, result_ref,
     hot_ref, val_ref, req_ref, got_ref, east_ref, west_ref, left_ref, right_ref, top_ref, bottom_ref, corner_ref,
-    x_ref, tap8_ref, mix_ref, q_ref, row_ref, half_ref, idx_ref, where_ref, table_ref, w_ref, out_ref, ret_ref, wide_ref,
+    x_ref, tap8_ref, pack_ref, band_ref, part_ref, mix_ref, q_ref, row_ref, half_ref, idx_ref, where_ref, table_ref, w_ref, out_ref, ret_ref,
     x0_ref, x1_ref, idx_smem, row_smem,
     send_sem, recv_sem, req_send, req_recv, own_sem, val_send, val_recv, idx_sem, row_sem, *, n_lat, n_lon, turn, unroll):
     lat, lon = lax.axis_index("lat"), lax.axis_index("lon")
@@ -290,8 +329,10 @@
 
     lax.fori_loop(0, 12, relay, 0)
     for h in range(2):
-        for t in range(49):
-            tap8_ref[h, t * 8:(t + 1) * 8, :] = jnp.broadcast_to(tap_ref[t:t + 1, h * 128:(h + 1) * 128].astype(F32), (8, 128))
+        for t in range(7 * SPLIT, 49):
+            tap8_ref[h, t * 8:(t + 1) * 8, :] = jnp.broadcast_to(tap_ref[t // 7, t % 7:t % 7 + 1, h * 128:(h + 1) * 128].astype(F32), (8, 128))
+
+    tap_bands(tap_ref, band_ref)
 
     for h in halos:
         h.wait()
@@ -329,7 +370,8 @@
             v = corner_ref[n, (r - 7) // 2 * 16:(r - 7) // 2 * 16 + 16, :].astype(F32) * below
             put_side(r, 7, v[(r - 7) % 2 * 8:(r - 7) % 2 * 8 + 8], c)
 
-    grid_body(x_ref, tap8_ref, mix_ref, gain_ref, up_ref, down_ref, read_ref, q_ref, first, tile_rows * n_lat)
+    pack_pairs(x_ref, pack_ref)
+    grid_body(x_ref, tap8_ref, pack_ref, band_ref, part_ref, mix_ref, gain_ref, up_ref, down_ref, read_ref, q_ref, first, tile_rows * n_lat)
 
     own.wait()
     most = pl.ds(0, (devices - 1) * 8)
@@ -347,34 +389,48 @@
 
     low = lax.broadcasted_iota(I32, (32, 128), 1) < 64
 
+    share = devices // 8
+
     def rows(d):
         return pl.ds(pl.multiple_of(d * 64, 64), 64)
 
     mine = pltpu.make_async_copy(out_ref.at[rows(me)], ret_ref.at[rows(me)], own_sem)
 
-    def send(d, to):
+    def send(d, to, group):
         pltpu.make_async_remote_copy(
-            src_ref=out_ref.at[rows(d)], dst_ref=ret_ref.at[rows(me)], send_sem=val_send, recv_sem=val_recv,
+            src_ref=out_ref.at[rows(d)], dst_ref=ret_ref.at[rows(me)], send_sem=val_send, recv_sem=val_recv.at[group],
             device_id=to, device_id_type=pl.DeviceIdType.MESH).start()
 
     def serve(j, _):
-        for u in range(unroll):
-            d, to = partner(j * unroll + u)
+        those = [partner(j * unroll + u) for u in range(unroll)]
+        for d, _ in those:
             read_source(idx_smem, d, table_ref, w_ref, out_ref, low)
-            if u:
-                send(d, to)
-            else:
-                pl.when(j > 0)(functools.partial(send, d, to))
-                pl.when(j == 0)(mine.start)
+        group = lax.div(j * unroll, share)
+        pl.when(j > 0)(functools.partial(send, *those[0], group))
+        pl.when(j == 0)(mine.start)
+        for d, to in those[1:]:
+            send(d, to, group)
         return 0
 
     lax.fori_loop(0, devices // unroll, serve, 0)
-    mine.wait()
+    wide_ref = x_ref.at[0]
+    for group in range(devices // share):
+        count = pl.ds(0, (share - (group == 0)) * 64)
+        pltpu.make_async_copy(out_ref.at[count], ret_ref.at[count], val_recv.at[group]).wait()
+        if group == 0:
+            mine.wait()
+
+        def widen(k, _):
+            s = lax.rem(me + (devices - k) * turn, devices)
+            wide_ref[rows(s), :] = ret_ref[rows(s), :].astype(F32)
+            return 0
+
+        lax.fori_loop(group * share, (group + 1) * share, widen, 0)
+
     rows_in.wait()
     most = pl.ds(0, (devices - 1) * 64)
     pltpu.make_async_copy(out_ref.at[most], ret_ref.at[most], val_send).wait()
-    pltpu.make_async_copy(out_ref.at[most], ret_ref.at[most], val_recv).wait()
-    place_body(row_smem, half_ref, ret_ref, result_ref, wide_ref, x0_ref, x1_ref)
+    place_body(row_smem, half_ref, wide_ref, result_ref, x0_ref, x1_ref)
 
 
 def window(owner, offsets, fractions, grid, taps, gain, up, down, read2, n_lat, n_lon):
@@ -392,23 +448,24 @@
             VM((128, 1024), BF16), VM((768, 1024), BF16), VM((devices * 8, 128), F32), VM((devices * 8, 128), F32),
             VM((pairs * 16, 256), BF16), VM((pairs * 16, 256), BF16), VM((pairs * 16, 256), BF16), VM((pairs * 16, 256), BF16),
             VM((4, tile_cols, 256), BF16), VM((5, tile_cols, 256), BF16), VM((4, 48, 256), BF16),
-            VM((2, 12 * EXT * 8, 128), F32), VM((2, 49 * 8, 128), F32), VM((6 * COLS * 8, 256), F32),
+            VM((2, 12 * EXT * 8, 128), F32), VM((2, 49 * 8, 128), F32),
+            VM((2, 2, 2, 12, PAIRS * 8 + 32, 128), BF16), VM((2, SPLIT, 1024, 256), BF16), VM((2, PAIRS * 8, 128), F32),
+            VM((6, PAIRS, 2, 8, 256), F32),
             VM((6 * COLS * 8, 128), F32), VM((n, 128), I32), VM((n, 128), I32), VM((devices, 128), I32), VM((2, devices, 128), F32),
             VM((tile_rows * tile_cols, 8, 128), F32), VM((2, devices, 1024), F32), VM((devices * 64, 128), BF16),
-            VM((devices * 64, 128), BF16), VM((devices * 64, 128), F32), VM((128, 128), F32), VM((128, 128), F32),
+            VM((devices * 64, 128), BF16), VM((128, 128), F32), VM((128, 128), F32),
             pltpu.SMEM((devices, 128), I32), pltpu.SMEM((n, 128), I32),
-            dma((8,)), dma((8,)), dma, dma, dma, dma, dma, dma, dma],
-        compiler_params=pltpu.CompilerParams(vmem_limit_bytes=60 << 20, has_side_effects=True, collective_id=0),
+            dma((8,)), dma((8,)), dma, dma, dma, dma, dma((8,)), dma, dma],
+        compiler_params=pltpu.CompilerParams(vmem_limit_bytes=62 << 20, has_side_effects=True, collective_id=0),
         name="window",
     )(owner.reshape(n, 128), offsets.reshape(n, 128), fractions, grid, taps, gain, up, down, read2)
 
 
 def shards(grid, dw_kernel, norm_gain, w_up, w_down, w_read, owner, offsets, fractions):
     n_lat, n_lon = lax.axis_size("lat"), lax.axis_size("lon")
-    read = w_read.T
     return window(
-        owner, offsets, fractions, grid, dw_kernel.reshape(49, -1), norm_gain, w_up[0], w_down[0],
-        jnp.concatenate([read, read], axis=0), n_lat, n_lon).T
+        owner, offsets, fractions, grid, dw_kernel[0], norm_gain, w_up[0], w_down[0],
+        w_read.T, n_lat, n_lon).T
 
 
 def solution(mesh):

time: 125 us -> 97.3 us (0.78)
  Pallas kernels: 120 us -> 94.9 us
  other arithmetic: 1.47 us -> 0 us
  local copies, waits for them, and re-layouts: 3.63 us -> 2.26 us
    pallas_call x1, Pallas kernels: 120 us -> 94.9 us  [window(): pl.pallas_call(functools.partial(window_kernel, n_lat=n_lat, n_lon=n_lon,...]
    concatenate x1 -> x0, other arithmetic: 1.47 us -> none  [shards(): jnp.concatenate([read, read], axis=0)]
    reshape x1 -> x0, local copies, waits for them, and re-layouts: 1.37 us -> none  [shards(): dw_kernel.reshape(49, -1)]
where the time goes in v4:
time: 97.3 us; the launch traced here: 97.1 us
  Pallas kernels  94.9 us (98%)
  local copies, waits for them, and re-layouts  2.26 us (2%)
    pallas_call x1, Pallas kernels, window(): pl.pallas_call(functools.partial(window_kernel, n_lat=n_lat, n_lon=n_lon,...  94.9 us
    unnamed x1, local copies, waits for them, and re-layouts  2.26 us

profile of v4, /device:TPU:1, one launch (start us, length us, event | category | flops | bytes accessed | tf_op | source)
XLA Modules:
  0.0 97.1 jit_solution(10733799343240158373)
XLA Ops:
  0.0 94.9 %window.1 = bf16[64,8192]{1,0:T(8,128)(2,1)} custom-call(s32[64,128]{1,0:T(8,128)} %bitcast.10, s32[64,128]{1,0:T(8,128)} %bitcast.11, f32[2,8192]{1,0:T(2,128)} %fr_ref.1, bf16[45,90,256]{2,1,0:T(8,128)(2,1)} %grid_ref.1, bf16[7,7,256]{2,1,0:T(8,128)(2,1)} %bitcast.13, f32[1,256]{1,0:T(1,128)} %gain_ref.1, bf16[256,512]{1,0:T(8,128)(2,1)} %bitcast.8, ...), custom_call_target="tpu_custom_call" | custom-call | tf_op jit(solution)/shard_map/window/pallas_call | solution.py:442
  94.9 2.3 %copy.11 = bf16[8192,64]{0,1:T(8,128)(2,1)} copy(bf16[8192,64]{0,1:T(8,128)(2,1)} %bitcast.7) | data formatting | bytes 2097152

commit v5 on v4

--- a/solution.py
+++ b/solution.py
@@ -12,13 +12,13 @@
 SPLIT = 3
 
 
-def route_body(owner_ref, off_ref, fr_ref, req_ref, row_ref, half_ref, hot_ref, val_ref):
+def route_body(owner_ref, off_ref, fr_ref, req_ref, row_ref, half_ref, hot_ref, val_ref, sum_ref):
     blocks = owner_ref.shape[0]
     sub = lax.broadcasted_iota(I32, (128, 128), 0)
     lane = lax.broadcasted_iota(I32, (128, 128), 1)
     upper = jnp.where(sub < lane, 1.0, 0.0).astype(BF16)
     prefix = jnp.concatenate([upper, jnp.ones((128, 128), BF16)], axis=1)
-    group = 8
+    group = 16
 
     def step(k, base):
         for u in range(group):
@@ -42,14 +42,15 @@
             parts = [(off >> 6).astype(F32), (off & 63).astype(F32), fy_hi, fy - fy_hi, fx_hi, fx - fx_hi]
             for p, part in enumerate(parts):
                 val_ref[p * 128:(p + 1) * 128, u * 128:(u + 1) * 128] = jnp.where(there, part, 0.0).astype(BF16)
-        acc = lax.dot_general(hot_ref[...], val_ref[...], (((1,), (1,)), ((), ())), preferred_element_type=F32)
-        new = [acc[:, 0:128] * 64.0 + acc[:, 128:256], acc[:, 256:384] + acc[:, 384:512], acc[:, 512:640] + acc[:, 640:768]]
+        acc = lax.dot_general(val_ref[...], hot_ref[...], (((1,), (1,)), ((), ())), preferred_element_type=F32)
+        new = [acc[0:128] * 64.0 + acc[128:256], acc[256:384] + acc[384:512], acc[512:640] + acc[640:768]]
         for q in range(3):
-            at = pl.ds(q, 128, stride=8)
-            req_ref[at, :] = jnp.where(k == 0, new[q], req_ref[at, :] + new[q])
+            sum_ref[q] = jnp.where(k == 0, new[q], sum_ref[q] + new[q])
         return base
 
     lax.fori_loop(0, blocks // group, step, jnp.zeros((128, 128), F32))
+    for q in range(3):
+        req_ref[pl.ds(q, 128, stride=8), :] = jnp.transpose(sum_ref[q])
 
 
 def tap_bands(tap_ref, band_ref):
@@ -151,10 +152,11 @@
     col = lax.broadcasted_iota(I32, (128, 1024), 1)
     for s in range(8):
         one = jnp.where(col == row * 8 + s, 1.0, 0.0).astype(BF16)
+        planes = [(a[s // 2] * b[2 * (s % 2) + half]).astype(BF16) for half in range(2)]
+        part = jnp.dot(jnp.concatenate(planes, axis=0), one, preferred_element_type=F32)
         for half in range(2):
-            plane = (a[s // 2] * b[2 * (s % 2) + half]).astype(BF16)
-            part = jnp.dot(plane, one, preferred_element_type=F32)
-            w_ref[half] = part if s == 0 else w_ref[half] + part
+            own = part[half * 128:(half + 1) * 128]
+            w_ref[half] = own if s == 0 else w_ref[half] + own
 
 
 def build_table(q_ref, table_ref, tile_rows, tile_cols):
@@ -229,11 +231,11 @@
 
 
 def window_kernel(
-    owner_ref, off_ref, fr_ref, grid_ref, tap_ref, gain_ref, up_ref, down_ref, read_ref, result_ref,
-    hot_ref, val_ref, req_ref, got_ref, east_ref, west_ref, left_ref, right_ref, top_ref, bottom_ref, corner_ref,
+    owner_ref, off_ref, fr_ref, grid_hbm, tap_ref, gain_ref, up_ref, down_ref, read_ref, result_ref,
+    grid_ref, hot_ref, val_ref, sum_ref, req_ref, got_ref, east_ref, west_ref, left_ref, right_ref, top_ref, bottom_ref, corner_ref,
     x_ref, tap8_ref, pack_ref, band_ref, part_ref, mix_ref, q_ref, row_ref, half_ref, idx_ref, where_ref, table_ref, w_ref, out_ref, ret_ref,
     x0_ref, x1_ref, idx_smem, row_smem,
-    send_sem, recv_sem, req_send, req_recv, own_sem, val_send, val_recv, idx_sem, row_sem, *, n_lat, n_lon, turn, unroll):
+    send_sem, recv_sem, req_send, req_recv, own_sem, val_send, val_recv, idx_sem, row_sem, grid_sem, line_sem, *, n_lat, n_lon, turn, unroll):
     lat, lon = lax.axis_index("lat"), lax.axis_index("lon")
     me = lat * n_lon + lon
     devices = n_lat * n_lon
@@ -246,22 +248,17 @@
 
     barrier = pltpu.get_barrier_semaphore()
 
-    def hello(k, _):
-        pl.semaphore_signal(barrier, inc=1, device_id=partner(k)[1], device_id_type=pl.DeviceIdType.MESH)
-        return 0
-
-    lax.fori_loop(1, devices, hello, 0)
-
-    def pack(k, _):
-        a = grid_ref[2 * k].astype(F32)
-        b = grid_ref[jnp.minimum(2 * k + 1, tile_rows - 1)].astype(F32)
-        at = pl.ds(pl.multiple_of(k * 16, 16), 16)
-        east_ref[at, :] = jnp.concatenate([a[tile_cols - 8:], b[tile_cols - 8:]], axis=0).astype(BF16)
-        west_ref[at, :] = jnp.concatenate([a[:8], b[:8]], axis=0).astype(BF16)
-        return 0
+    def greet(sem, to):
+        pl.semaphore_signal(sem, inc=1, device_id=to, device_id_type=pl.DeviceIdType.MESH)
+
+    for k in range(1, n_lon):
+        greet(barrier, (lat, lax.rem(lon + k, n_lon)))
+    for k in range(1, n_lat):
+        greet(barrier, (lax.rem(lat + k, n_lat), lon))
+    grid_in = pltpu.make_async_copy(grid_hbm, grid_ref, grid_sem)
+    grid_in.start()
 
     pairs = (tile_rows + 1) // 2
-    lax.fori_loop(0, pairs, pack, 0)
     up = lax.rem(lat + n_lat - 1, n_lat)
     down = lax.rem(lat + 1, n_lat)
     prev = lax.rem(lon + n_lon - 1, n_lon)
@@ -282,10 +279,54 @@
                                      device_id_type=pl.DeviceIdType.MESH)
         for n, (a, b, to) in enumerate(moves)
     ]
-    route_body(owner_ref, off_ref, fr_ref, req_ref, row_ref, half_ref, hot_ref, val_ref)
+    route_body(owner_ref, off_ref, fr_ref, req_ref, row_ref, half_ref, hot_ref, val_ref, sum_ref)
     rows_in = pltpu.make_async_copy(row_ref, row_smem, row_sem)
     rows_in.start()
-    pl.semaphore_wait(barrier, devices - 1)
+    pl.semaphore_wait(barrier, n_lat + n_lon - 2)
+    for k in range(1, n_lat):
+        greet(line_sem, (lax.rem(lat + k, n_lat), lon))
+    grid_in.wait()
+    def pack(k, _):
+        a = grid_ref[2 * k].astype(F32)
+        b = grid_ref[jnp.minimum(2 * k + 1, tile_rows - 1)].astype(F32)
+        at = pl.ds(pl.multiple_of(k * 16, 16), 16)
+        east_ref[at, :] = jnp.concatenate([a[tile_cols - 8:], b[tile_cols - 8:]], axis=0).astype(BF16)
+        west_ref[at, :] = jnp.concatenate([a[:8], b[:8]], axis=0).astype(BF16)
+        return 0
+
+    lax.fori_loop(0, pairs, pack, 0)
+
+    def put(h, r, c, s, v):
+        x_ref[h, pl.ds((r * EXT + c) * 8 + s, v.shape[0], stride=8), :] = v
+
+    def put_row(r, s, v):
+        for h in range(2):
+            for c in range(0, tile_cols, 8):
+                put(h, r, c + 8, s, v[c:min(c + 8, tile_cols), h * 128:(h + 1) * 128])
+
+    def put_side(r, s, v, c):
+        for h in range(2):
+            put(h, r, c, s, v[:, h * 128:(h + 1) * 128])
+
+    for r in range(12):
+        if r >= 4:
+            put_row(r, 0, grid_ref[r - 4].astype(F32))
+        if r <= tile_rows - 39:
+            put_row(r, 7, grid_ref[38 + r].astype(F32))
+
+    def relay(r, _):
+        for s in range(1, 7):
+            put_row(r, s, grid_ref[6 * s + r - 4].astype(F32))
+        return 0
+
+    lax.fori_loop(0, 12, relay, 0)
+    for h in range(2):
+        for t in range(7 * SPLIT, 49):
+            tap8_ref[h, t * 8:(t + 1) * 8, :] = jnp.broadcast_to(tap_ref[t // 7, t % 7:t % 7 + 1, h * 128:(h + 1) * 128].astype(F32), (8, 128))
+
+    tap_bands(tap_ref, band_ref)
+
+    pl.semaphore_wait(line_sem, n_lat - 1)
     for h in halos:
         h.start()
 
@@ -303,36 +344,6 @@
         return 0
 
     lax.fori_loop(1, devices, ask, 0)
-
-    def put(h, r, c, s, v):
-        x_ref[h, pl.ds((r * EXT + c) * 8 + s, v.shape[0], stride=8), :] = v
-
-    def put_row(r, s, v):
-        for h in range(2):
-            for c in range(0, tile_cols, 8):
-                put(h, r, c + 8, s, v[c:min(c + 8, tile_cols), h * 128:(h + 1) * 128])
-
-    def put_side(r, s, v, c):
-        for h in range(2):
-            put(h, r, c, s, v[:, h * 128:(h + 1) * 128])
-
-    for r in range(12):
-        if r >= 4:
-            put_row(r, 0, grid_ref[r - 4].astype(F32))
-        if r <= tile_rows - 39:
-            put_row(r, 7, grid_ref[38 + r].astype(F32))
-
-    def relay(r, _):
-        for s in range(1, 7):
-            put_row(r, s, grid_ref[6 * s + r - 4].astype(F32))
-        return 0
-
-    lax.fori_loop(0, 12, relay, 0)
-    for h in range(2):
-        for t in range(7 * SPLIT, 49):
-            tap8_ref[h, t * 8:(t + 1) * 8, :] = jnp.broadcast_to(tap_ref[t // 7, t % 7:t % 7 + 1, h * 128:(h + 1) * 128].astype(F32), (8, 128))
-
-    tap_bands(tap_ref, band_ref)
 
     for h in halos:
         h.wait()
@@ -442,10 +453,10 @@
     return pl.pallas_call(
         functools.partial(window_kernel, n_lat=n_lat, n_lon=n_lon, turn=37, unroll=8),
         out_shape=jax.ShapeDtypeStruct((64, n * 128), BF16),
-        in_specs=[pl.BlockSpec(memory_space=VM)] * 9,
+        in_specs=[pl.BlockSpec(memory_space=pl.ANY if k == 3 else VM) for k in range(9)],
         out_specs=pl.BlockSpec(memory_space=VM),
         scratch_shapes=[
-            VM((128, 1024), BF16), VM((768, 1024), BF16), VM((devices * 8, 128), F32), VM((devices * 8, 128), F32),
+            VM(grid.shape, BF16), VM((128, 2048), BF16), VM((768, 2048), BF16), VM((3, 128, 128), F32), VM((devices * 8, 128), F32), VM((devices * 8, 128), F32),
             VM((pairs * 16, 256), BF16), VM((pairs * 16, 256), BF16), VM((pairs * 16, 256), BF16), VM((pairs * 16, 256), BF16),
             VM((4, tile_cols, 256), BF16), VM((5, tile_cols, 256), BF16), VM((4, 48, 256), BF16),
             VM((2, 12 * EXT * 8, 128), F32), VM((2, 49 * 8, 128), F32),
@@ -455,8 +466,8 @@
             VM((tile_rows * tile_cols, 8, 128), F32), VM((2, devices, 1024), F32), VM((devices * 64, 128), BF16),
             VM((devices * 64, 128), BF16), VM((128, 128), F32), VM((128, 128), F32),
             pltpu.SMEM((devices, 128), I32), pltpu.SMEM((n, 128), I32),
-            dma((8,)), dma((8,)), dma, dma, dma, dma, dma((8,)), dma, dma],
-        compiler_params=pltpu.CompilerParams(vmem_limit_bytes=62 << 20, has_side_effects=True, collective_id=0),
+            dma((8,)), dma((8,)), dma, dma, dma, dma, dma((8,)), dma, dma, dma, pltpu.SemaphoreType.REGULAR],
+        compiler_params=pltpu.CompilerParams(vmem_limit_bytes=63 << 20, has_side_effects=True, collective_id=0),
         name="window",
     )(owner.reshape(n, 128), offsets.reshape(n, 128), fractions, grid, taps, gain, up, down, read2)
 

time: 97.3 us -> 95.1 us (0.977)
  Pallas kernels: 94.9 us -> 92.6 us
    pallas_call x1, Pallas kernels: 94.9 us -> 92.6 us  [window(): pl.pallas_call(functools.partial(window_kernel, n_lat=n_lat, n_lon=n_lon,...]
where the time goes in v5:
time: 95.1 us; the launch traced here: 94.9 us
  Pallas kernels  92.6 us (97%)
  local copies, waits for them, and re-layouts  2.26 us (2%)
    pallas_call x1, Pallas kernels, window(): pl.pallas_call(functools.partial(window_kernel, n_lat=n_lat, n_lon=n_lon,...  92.6 us
    unnamed x1, local copies, waits for them, and re-layouts  2.26 us

profile of v5, /device:TPU:1, one launch (start us, length us, event | category | flops | bytes accessed | tf_op | source)
XLA Modules:
  0.0 94.9 jit_solution(17729944852913930524)
XLA Ops:
  0.0 92.6 %window.1 = bf16[64,8192]{1,0:T(8,128)(2,1)} custom-call(s32[64,128]{1,0:T(8,128)} %bitcast.10, s32[64,128]{1,0:T(8,128)} %bitcast.11, f32[2,8192]{1,0:T(2,128)} %fr_ref.1, bf16[45,90,256]{2,1,0:T(8,128)(2,1)} %grid_hbm.1, bf16[7,7,256]{2,1,0:T(8,128)(2,1)} %bitcast.13, f32[1,256]{1,0:T(1,128)} %gain_ref.1, bf16[256,512]{1,0:T(8,128)(2,1)} %bitcast.8, ...), custom_call_target="tpu_custom_call" | custom-call | tf_op jit(solution)/shard_map/window/pallas_call | solution.py:453
  92.6 2.3 %copy.11 = bf16[8192,64]{0,1:T(8,128)(2,1)} copy(bf16[8192,64]{0,1:T(8,128)(2,1)} %bitcast.7) | data formatting | bytes 2097152
